TPU v7x, 128 devices: a whole 4x4x4 slice. The times are simulated.
128 devices in a mesh: pool: 32 (over y, x, core), tensor: 4 (over z).
Axes of the slice: x: 4, y: 4, z: 4, core: 2. Of those that a mesh axis runs over, the one named last changes fastest.
Arguments:
- store: bfloat16 [384, 128, 5120], P('pool', None, 'tensor'), may hold values from -60 to 60
- new_hidden: bfloat16 [4096, 5120], P('pool', 'tensor'), may hold values from -60 to 60
- wq: bfloat16 [5120, 4096], P(None, 'tensor'), may hold values from -0.078125 to 0.078125
- wk: bfloat16 [5120, 1024], P(None, 'tensor'), may hold values from -0.078125 to 0.078125
- wv: bfloat16 [5120, 1024], P(None, 'tensor'), may hold values from -0.078125 to 0.078125
- norm_gain: float32 [5120], replicated, may hold values from 0.1 to 1.9
- q_gain: float32 [128], replicated, may hold values from 1 to 2
- k_gain: float32 [128], replicated, may hold values from 1 to 2
- page_table: int32 [32, 16], replicated, may hold values from -1 to 383, as said below
- hist_len: int32 [32], replicated, may hold values from 1 to 2048, as said below
Outputs:
- context: bfloat16 [4096, 4096], P('pool', 'tensor')
Inputs may be any that keep to these rules, and one draw needn't show every extreme that they name: `page_table`: row r lists request r's history pages in order; its first ceil(hist_len[r] / 128) entries are page ids (owner id // 12, slot id % 12) and the rest are -1. Every page id appears exactly once in the table, and no request holds two pages of one owner. `hist_len`: some request has 16 full pages.
All inputs are finite; a program needn't handle non-finite values.
Results may differ from a plain program's by a relative error of at most 0.012.
Values may be sent and summed in bfloat16 or wider, within the bound.
A program may use at most 192 MiB of HBM per device.

v0:
```python
import jax
import jax.numpy as jnp
from jax import lax
from jax.sharding import PartitionSpec as P

epsilon = 1e-06
rope_base = 1000000.0


def rms_rows(row_block, gain_vec):
    values = row_block.astype(jnp.float32)
    inv_rms = lax.rsqrt(jnp.mean(values * values, axis=-1, keepdims=True) + epsilon)
    return (values * inv_rms * gain_vec).astype(jnp.bfloat16)


def head_norm(values, gain_vec):
    inv_rms = lax.rsqrt(jnp.mean(values * values, axis=-1, keepdims=True) + epsilon)
    return values * inv_rms * gain_vec


def rotate(values, positions):
    half_width = values.shape[-1] // 2
    exponent = jnp.arange(half_width, dtype=jnp.float32) * (2.0 / values.shape[-1])
    frequency = jnp.power(jnp.float32(rope_base), -exponent)
    angles = positions.astype(jnp.float32)[:, None] * frequency[None, :]
    cosine = jnp.cos(angles)[:, None, :]
    sine_part = jnp.sin(angles)[:, None, :]
    first = values[..., :half_width]
    second = values[..., half_width:]
    return jnp.concatenate(
        [first * cosine - second * sine_part, second * cosine + first * sine_part], axis=-1
    )


def project_pages(row_block, positions, norm_gain, wk, wv, k_gain, head_count, head_size):
    normed = rms_rows(row_block, norm_gain)
    raw_keys = jnp.dot(normed, wk, preferred_element_type=jnp.float32).reshape(
        -1, head_count, head_size
    )
    key_rows = rotate(head_norm(raw_keys, k_gain), positions).astype(jnp.bfloat16)
    value_rows = (
        jnp.dot(normed, wv, preferred_element_type=jnp.float32)
        .astype(jnp.bfloat16)
        .reshape(-1, head_count, head_size)
    )
    return (key_rows, value_rows)


def local(store, new_hidden, wq, wk, wv, norm_gain, q_gain, k_gain, page_table, hist_len):
    page_count = store.shape[0]
    page_rows = store.shape[1]
    slot_total = page_table.shape[1]
    head_size = q_gain.shape[0]
    local_kv = wk.shape[1] // head_size
    local_q = wq.shape[1] // head_size
    new_count = new_hidden.shape[0]
    history = slot_total * page_rows
    position = lax.axis_index("pool")
    owner_ids = jnp.where(page_table >= 0, page_table // page_count, -1)
    slot_ids = jnp.where(page_table >= 0, page_table % page_count, 0)
    owned_here = owner_ids == position
    holding = jnp.any(owned_here, axis=1)
    send_slot = jnp.sum(jnp.where(owned_here, slot_ids, 0), axis=1)
    my_pages = lax.dynamic_index_in_dim(page_table, position, 0, keepdims=False)
    source = jnp.maximum(my_pages // page_count, 0)
    length = lax.dynamic_index_in_dim(hist_len, position, 0, keepdims=False)
    whole_new = lax.all_gather(new_hidden, "tensor", axis=1, tiled=True)
    new_normed = rms_rows(whole_new, norm_gain)
    new_pos = length + jnp.arange(new_count, dtype=jnp.int32)
    raw_queries = jnp.dot(new_normed, wq, preferred_element_type=jnp.float32).reshape(
        new_count, local_q, head_size
    )
    queries = rotate(head_norm(raw_queries, q_gain), new_pos).astype(jnp.bfloat16)
    raw_new_keys = jnp.dot(new_normed, wk, preferred_element_type=jnp.float32).reshape(
        new_count, local_kv, head_size
    )
    keys_new = rotate(head_norm(raw_new_keys, k_gain), new_pos).astype(jnp.bfloat16)
    values_new = (
        jnp.dot(new_normed, wv, preferred_element_type=jnp.float32)
        .astype(jnp.bfloat16)
        .reshape(new_count, local_kv, head_size)
    )
    chosen = jnp.take(store, send_slot, axis=0)
    outgoing = jnp.where(holding[:, None, None], chosen, jnp.zeros_like(chosen))
    arrived = lax.all_to_all(outgoing, "pool", split_axis=0, concat_axis=0, tiled=True)
    ordered = jnp.take(arrived, source, axis=0)
    whole_hist = lax.all_gather(ordered, "tensor", axis=2, tiled=True)
    hist_pos = jnp.arange(history, dtype=jnp.int32)
    keys_hist, values_hist = project_pages(
        whole_hist.reshape(history, -1), hist_pos, norm_gain, wk, wv, k_gain, local_kv, head_size
    )
    key_rows = jnp.concatenate([keys_hist, keys_new], axis=0)
    value_rows = jnp.concatenate([values_hist, values_new], axis=0)
    grouped = queries.reshape(new_count, local_kv, local_q // local_kv, head_size)
    scores = jnp.einsum(
        "qkgd,skd->kgqs", grouped, key_rows, preferred_element_type=jnp.float32
    ) * head_size ** (-0.5)
    key_index = jnp.arange(history + new_count, dtype=jnp.int32)[None, :]
    query_index = jnp.arange(new_count, dtype=jnp.int32)[:, None]
    allowed = jnp.where(key_index < history, key_index < length, key_index - history <= query_index)
    raw = jnp.where(allowed, jnp.exp(scores), jnp.float32(0.0))
    denominator = jnp.sum(raw, axis=-1, keepdims=True)
    weights = (raw / denominator).astype(jnp.bfloat16)
    mixed = jnp.einsum("kgqs,skd->qkgd", weights, value_rows, preferred_element_type=jnp.float32)
    return mixed.reshape(new_count, local_q * head_size).astype(jnp.bfloat16)


def solution(mesh):
    return jax.shard_map(
        local,
        mesh=mesh,
        in_specs=(
            P("pool", None, "tensor"),
            P("pool", "tensor"),
            P(None, "tensor"),
            P(None, "tensor"),
            P(None, "tensor"),
            P(),
            P(),
            P(),
            P(),
            P(),
        ),
        out_specs=P("pool", "tensor"),
        check_vma=False,
    )
```

profile of v0, /device:TPU:1, one launch (start us, length us, event | category | flops | bytes accessed | tf_op | source)
XLA Modules:
  0.0 434.7 jit_solution(12217165087614661446)
XLA Ops:
  6.5 0.9 fusion.43
  7.4 0.7 fusion.25
  8.2 7.8 %gather_fusion = bf16[32,128,1280]{2,1,0:T(8,128)(2,1)} fusion(bf16[12,128,1280]{2,1,0:T(8,128)(2,1)} %param.10, s32[1024]{0:T(1024)S(1)} %pad_clamp_fusion.1), kind=kCustom, calls=%fused_computation | custom fusion | bytes 20971648 | tf_op jit(solution)/shard_map/jit(_take)/gather | solution.py:83
  16.0 10.3 %select_select_fusion = bf16[32,128,1280]{2,1,0:T(8,128)(2,1)} fusion(bf16[32,128,1280]{2,1,0:T(8,128)(2,1)} %gather_fusion, pred[32]{0:T(512)(128)(4,1)S(1)} %compare_and_fusion, pred[32]{0:T(512)(128)(4,1)S(1)} %get-tuple-element.5), kind=kLoop, calls=%fused_computation.7 | loop fusion | flops 10485760 | bytes 20971584 | tf_op jit(solution)/shard_map/jit(_where)/select_n | solution.py:84
  26.3 8.8 %all-to-all-start = ((bf16[32,128,1280]{2,1,0:T(8,128)(2,1)}), bf16[32,128,1280]{2,1,0:T(8,128)(2,1)}, u32[]{:S(2)}, u32[]{:S(2)}) async-start(bf16[32,128,1280]{2,1,0:T(8,128)(2,1)} %select_select_fusion), calls=%async_computation | async-start | bytes 20971520 | tf_op jit(solution)/shard_map/all_to_all | solution.py:85
  35.1 0.0 all-gather.5.cloned.1.call-start
  35.2 0.7 all-gather.5.cloned.1.call-update
  35.9 0.2 fusion.28
  36.1 0.2 divide_reduce_fusion
  36.4 124.8 %all-to-all-done = bf16[32,128,1280]{2,1,0:T(8,128)(2,1)} async-done(((bf16[32,128,1280]{2,1,0:T(8,128)(2,1)}), bf16[32,128,1280]{2,1,0:T(8,128)(2,1)}, u32[]{:S(2)}, u32[]{:S(2)}) %all-to-all-start) | async-done | bytes 10485792 | tf_op jit(solution)/shard_map/all_to_all | solution.py:85
  161.1 7.2 %gather_fusion.1 = bf16[16,128,1280]{2,1,0:T(8,128)(2,1)} fusion(bf16[32,128,1280]{2,1,0:T(8,128)(2,1)} %all-to-all-done, s32[1024]{0:T(1024)S(1)} %pad_clamp_fusion), kind=kCustom, calls=%fused_computation.1 | custom fusion | bytes 10485824 | tf_op jit(solution)/shard_map/jit(_take)/gather | solution.py:86
  168.3 5.4 %broadcast_select_fusion = bf16[16,128,1280]{2,1,0:T(8,128)(2,1)} fusion(bf16[16,128,1280]{2,1,0:T(8,128)(2,1)} %gather_fusion.1, pred[16]{0:T(512)(128)(4,1)S(1)} %fusion.33), kind=kLoop, calls=%fused_computation.11 | loop fusion | flops 2621440 | bytes 10485776 | tf_op jit(solution)/shard_map/jit(_take)/select_n | solution.py:86
  173.7 4.4 %copy.59 = bf16[256,5120]{1,0:T(8,128)(2,1)} copy(bf16[256,5120]{0,1:T(8,128)(2,1)} %bitcast.74) | data formatting | bytes 5242880 | tf_op jit(solution)/shard_map/dot_general | solution.py:37
  178.2 0.6 dynamic_slice.9
  178.7 0.7 add_convert_fusion.3
  179.4 0.2 multiply_cosine_fusion.1
  179.6 0.7 copy.47
  180.3 0.7 copy.48
  181.1 0.7 iota_compare_fusion.1
  181.7 2.8 multiply_cosine_fusion
  184.5 1.8 fusion.17
  186.4 1.9 fusion.4
  188.3 8.4 %convolution_bitcast_fusion = f32[16,8,8,128]{3,1,2,0:T(8,128)S(1)} fusion(bf16[5120,1024]{1,0:T(8,128)(2,1)} %param.12, bf16[128,5120]{1,0:T(8,128)(2,1)} %all-gather.5.cloned.1.call-done, f32[5120]{0:T(1024)S(1)} %copy-done.7, f32[128]{0:T(128)S(1)} %add_rsqrt_fusion.4), kind=kOutput, calls=%fused_computation.21 | convolution fusion | flops 1344798720 | bytes 12341760 | tf_op jit(solution)/shard_map/dot_general | solution.py:70
  196.7 0.1 copy.62
  196.8 0.8 multiply_reduce_fusion.2
  197.6 0.9 copy.45
  198.5 0.8 copy.46
  199.3 1.2 multiply_multiply_fusion.1
  200.5 1.1 subtract_convert_fusion.1
  201.7 1.2 convolution_convert_fusion.1
  202.9 1.6 copy.58
  204.5 3.3 multiply_reduce_fusion.3
  207.8 0.1 multiply_multiply_fusion.2
  207.9 0.6 subtract_convert_fusion.2
  208.6 159.7 %all-gather.3.cloned.1.call-done = bf16[16,128,5120]{2,1,0:T(8,128)(2,1)} async-done(((bf16[16,128,1280]{2,1,0:T(8,128)(2,1)}), bf16[16,128,5120]{2,1,0:T(8,128)(2,1)}) %all-gather.3.cloned.1.call-update) | async-done | bytes 20971536 | tf_op jit(solution)/shard_map/all_gather | solution.py:87
  368.3 9.3 %multiply_reduce_fusion = f32[16,128]{1,0:T(8,128)S(1)} fusion(bf16[16,128,5120]{2,1,0:T(8,128)(2,1)} %all-gather.3.cloned.1.call-done), kind=kLoop, calls=%fused_computation.6 | loop fusion | flops 31455232 | bytes 20979712 | tf_op jit(solution)/shard_map/reduce_sum | solution.py:12
  377.5 3.9 copy-done.2
  381.4 10.6 %fusion.1 = bf16[2048,5120]{1,0:T(8,128)(2,1)} fusion(bf16[16,128,5120]{2,1,0:T(8,128)(2,1)S(1)} %copy-done.2, f32[5120]{0:T(1024)S(1)} %copy-done.7, f32[2048]{0:T(1024)S(1)} %get-tuple-element.15), kind=kLoop, calls=%fused_computation.4 | loop fusion | flops 41943040 | bytes 41971712 | tf_op jit(solution)/shard_map/convert_element_type | solution.py:13
  392.0 11.0 %convolution_convert_fusion = bf16[2048,256]{0,1:T(8,128)(2,1)} fusion(bf16[2048,5120]{1,0:T(8,128)(2,1)} %fusion.1, bf16[5120,256]{1,0:T(8,128)(2,1)S(1)} %copy-done), kind=kOutput, calls=%fused_computation.18 | convolution fusion | flops 5369233408 | bytes 24641536 | tf_op jit(solution)/shard_map/dot_general | solution.py:42
  403.0 12.3 %multiply_convert_fusion = bf16[16,128,5120]{2,1,0:T(8,128)(2,1)S(1)} fusion(bf16[16,128,5120]{2,1,0:T(8,128)(2,1)} %all-gather.3.cloned.1.call-done, f32[5120]{0:T(1024)S(1)} %copy-done.7, f32[16,128]{1,0:T(8,128)S(1)} %get-tuple-element.16), kind=kLoop, calls=%fused_computation.5 | loop fusion | flops 41943040 | bytes 41971712 | tf_op jit(solution)/shard_map/convert_element_type | solution.py:13
  415.3 5.6 %multiply_reduce_fusion.1 = (f32[2048,2]{0,1:T(2,128)S(1)}, f32[2048,2,128]{0,2,1:T(8,128)S(1)}) fusion(bf16[2048,5120,1]{1,0,2:T(8,128)(2,1)S(1)} %bitcast.72, bf16[2,128,5120]{2,1,0:T(8,128)(2,1)S(1)} %bitcast.75), kind=kOutput, calls=%fused_computation.20 | convolution fusion | flops 5369753600 | bytes 25706496 | tf_op jit(solution)/shard_map/dot_general | solution.py:37
  421.0 0.4 multiply_multiply_fusion
  421.4 0.6 copy-done.5
  422.0 0.2 copy-done.6
  422.2 0.3 subtract_convert_fusion
  422.5 2.3 fusion.2
  424.8 2.2 fusion.7
  427.0 0.9 copy.53
  (46 shorter events, 0.3 us)
Async XLA Ops:
  6.5 195.1 %copy-start = (bf16[5120,256]{1,0:T(8,128)(2,1)S(1)}, bf16[5120,256]{1,0:T(8,128)(2,1)}, u32[]{:S(2)}) copy-start(bf16[5120,256]{1,0:T(8,128)(2,1)} %param.14) | copy-start | bytes 7864324
  26.3 9.6 %copy-start.8 = (s32[32,16]{0,1:T(8,128)S(1)}, s32[32,16]{0,1:T(8,128)}, u32[]{:S(2)}) copy-start(s32[32,16]{0,1:T(8,128)} %param.18) | copy-start | bytes 6148
  26.3 134.8 %all-to-all-start = ((bf16[32,128,1280]{2,1,0:T(8,128)(2,1)}), bf16[32,128,1280]{2,1,0:T(8,128)(2,1)}, u32[]{:S(2)}, u32[]{:S(2)}) async-start(bf16[32,128,1280]{2,1,0:T(8,128)(2,1)} %select_select_fusion), calls=%async_computation | async-start | bytes 20971520 | tf_op jit(solution)/shard_map/all_to_all | solution.py:85
  35.1 151.2 %all-gather.5.cloned.1.call-start = ((), (), s32[]{:S(2)}) async-start(), calls=%async_computation.2 | async-start | bytes 1638400 | tf_op jit(solution)/shard_map/all_gather | solution.py:67
  35.9 332.4 %all-gather.3.cloned.1.call-start = ((), (), s32[]{:S(2)}) async-start(), calls=%async_computation.1 | async-start | bytes 26214400 | tf_op jit(solution)/shard_map/all_gather | solution.py:87
  173.7 4.5 %copy-start.13 = (s32[32]{0:T(128)S(1)}, s32[32]{0:T(128)}, u32[]{:S(2)}) copy-start(s32[32]{0:T(128)} %param.19) | copy-start | bytes 388
  178.1 10.1 %copy-start.7 = (f32[5120]{0:T(1024)S(1)}, f32[5120]{0:T(1024)}, u32[]{:S(2)}) copy-start(f32[5120]{0:T(1024)} %param.15) | copy-start | bytes 61444
  188.3 11.0 %copy-start.12 = (f32[128]{0:T(128)S(1)}, f32[128]{0:T(128)}, u32[]{:S(2)}) copy-start(f32[128]{0:T(128)} %param.16) | copy-start | bytes 1540
  199.3 2.4 copy-start.3
  202.9 4.9 %copy-start.11 = (f32[128]{0:T(128)S(1)}, f32[128]{0:T(128)}, u32[]{:S(2)}) copy-start(f32[128]{0:T(128)} %param.17) | copy-start | bytes 1540
  368.3 13.1 %copy-start.2 = (bf16[16,128,5120]{2,1,0:T(8,128)(2,1)S(1)}, bf16[16,128,5120]{2,1,0:T(8,128)(2,1)}, u32[]{:S(2)}) copy-start(bf16[16,128,5120]{2,1,0:T(8,128)(2,1)} %all-gather.3.cloned.1.call-done) | copy-start | bytes 62914564
  403.0 12.3 %copy-start.4 = (bf16[256,5120]{1,0:T(8,128)(2,1)S(1)}, bf16[256,5120]{1,0:T(8,128)(2,1)}, u32[]{:S(2)}) copy-start(bf16[256,5120]{1,0:T(8,128)(2,1)} %copy.59) | copy-start | bytes 7864324
  421.0 1.0 copy-start.5
  421.0 1.2 copy-start.6
  421.4 1.1 copy-start.10
  422.5 2.3 copy-start.9
  422.5 2.3 copy-start.14
  424.8 3.1 copy-start.1
Sparse Core Ops, SparseCore 0:
  37.6 26.0 all-gather.4
  173.8 194.4 all-gather.2
where the time goes:
time: 436 us; the launch traced here: 435 us
  waiting for transfers between devices  285 us (65%)
  other arithmetic  62.5 us (14%)
  matrix products  34 us (8%)
  local copies, waits for them, and re-layouts  30.4 us (7%)
  between operations  13.8 us (3%)
  starting transfers between devices  8.89 us (2%)
    all_gather x1, waiting for transfers between devices, local(): whole_hist = lax.all_gather(ordered, 'tensor', axis=2, tiled=True)  160 us
    all_to_all x1, waiting for transfers between devices, local(): lax.all_to_all(outgoing, 'pool', split_axis=0, concat_axis=0, tiled=True)  125 us
    convert_element_type x2, other arithmetic, rms_rows(): return (values * inv_rms * gain_vec).astype(jnp.bfloat16)  22.9 us
    reduce_sum x2, other arithmetic, rms_rows(): jnp.mean(values * values, axis=-1, keepdims=True) + epsilon  11.1 us
    dot_general x1, matrix products, project_pages(): jnp.dot(normed, wv, preferred_element_type=jnp.float32).astype(jnp.bfloat16)  11 us
    select_n x1, other arithmetic, local(): outgoing = jnp.where(holding[:, None, None], chosen, jnp.zeros_like(chosen))  10.3 us
    all_to_all x1, starting transfers between devices, local(): lax.all_to_all(outgoing, 'pool', split_axis=0, concat_axis=0, tiled=True)  8.81 us
  transfers between devices with their start and end apart: 3, of which 2 were waited for; matrix products, arithmetic and copies ran while one was open for 11% of the time, Pallas kernels for 0%

commit v1 on v0

v1 whole, which is shorter than its diff:
```python
import jax
import jax.numpy as jnp
import numpy as np
from jax import lax
from jax.experimental import pallas as pl
from jax.experimental.pallas import tpu as pltpu
from jax.sharding import PartitionSpec as P

EPS = 1e-06
ROPE_BASE = 1000000.0
MESH = pl.DeviceIdType.MESH
F32 = jnp.float32
BF16 = jnp.bfloat16

PAGES = 12
ROWS = 128
FEAT = 1280
NZ = 4
WIDE = FEAT * NZ
HD = 128
GROUP = 4
QROWS = GROUP * ROWS
REQS = 32
ITEMS = 12
HALF = 272
SEG = 160
SCALE = HD ** -0.5


def rope_tables():
    freq = ROPE_BASE ** (-np.arange(64, dtype=np.float64) * 2.0 / HD)
    freq = np.concatenate([freq, freq])[None, :]
    rows = np.arange(ROWS, dtype=np.float64)[:, None] * freq
    pages = np.arange(24, dtype=np.float64)[:, None] * ROWS * freq
    return [np.asarray(t, np.float32) for t in (np.cos(rows), np.sin(rows), np.cos(pages), np.sin(pages))]


class Ring:
    def __init__(self, piece, half, at, dev_up, dev_down, send, recv):
        self.piece, self.half, self.at = piece, half, at
        self.up, self.down, self.send, self.recv = dev_up, dev_down, send, recv
        self.left = lax.rem(at + 3, 4)
        self.right = lax.rem(at + 1, 4)
        self.opp = lax.rem(at + 2, 4)

    def copy(self, ref, k, dev):
        return pltpu.make_async_remote_copy(
            src_ref=ref, dst_ref=ref, send_sem=self.send(k), recv_sem=self.recv(k), device_id=dev, device_id_type=MESH
        )

    def start(self):
        self.copy(self.piece(self.at), 0, self.up).start()
        self.copy(self.piece(self.at), 1, self.down).start()

    def forward_left(self):
        self.copy(self.piece(self.left), 0, self.up).wait_recv()
        self.copy(self.half(self.left, 0), 2, self.up).start()

    def forward_right(self):
        self.copy(self.piece(self.right), 1, self.down).wait_recv()
        self.copy(self.half(self.right, 1), 3, self.down).start()

    def finish(self):
        self.copy(self.half(self.opp, 0), 2, self.up).wait_recv()
        self.copy(self.half(self.opp, 1), 3, self.down).wait_recv()

    def drain(self):
        self.copy(self.piece(self.at), 0, self.up).wait_send()
        self.copy(self.piece(self.at), 1, self.down).wait_send()
        self.copy(self.half(self.left, 0), 2, self.up).wait_send()
        self.copy(self.half(self.right, 1), 3, self.down).wait_send()


def nt(a, b):
    return lax.dot_general(a, b, (((1,), (1,)), ((), ())), preferred_element_type=F32)


def nn(a, b):
    return jnp.dot(a, b, preferred_element_type=F32)


def kernel(
    tab, store, new_hidden, wq, wk, wv, gain, q_gain, k_gain, cosr, sinr, cosp, sinp,
    out,
    X, W, WQB, WKB, WVB, ACC, NH, SSQ, INV, OPPS, OPPR, MIDS, MIDR, KB, VB, NEWCTX, QALL, CTX,
    S0, R0, S1O, R1O, S1M, R1M, A1, S2O, R2O, S2M, R2M, FIN,
    lsem, wbsem, w1s, w1r, w2s, w2r, w3s, w3r, nhs, nhr, sqs, sqr, os_, or_, ms, mr,
    q1s, q1r, q2s, q2r, q3s, q3r, c0s, c0r, c1os, c1or, c1ms, c1mr, c2os, c2or, c2ms, c2mr,
):
    p = lax.axis_index("pool")
    z = lax.axis_index("tensor")
    c = lax.rem(p, 2)
    x = lax.rem(p // 2, 4)
    y = p // 8
    oc = 1 - c

    def at(yy, xx, cc):
        return yy * 8 + xx * 2 + cc

    def rot(v, d):
        return lax.rem(v + d, 4)

    zdev = [(p, rot(z, d)) for d in range(4)]
    xup, xdn = (at(y, rot(x, 1), c), z), (at(y, rot(x, 3), c), z)
    yup, ydn = (at(rot(y, 1), x, c), z), (at(rot(y, 3), x, c), z)
    sib = (at(y, x, oc), z)

    def rcopy(src, dst, ss, rs, dev):
        return pltpu.make_async_remote_copy(
            src_ref=src, dst_ref=dst, send_sem=ss, recv_sem=rs, device_id=dev, device_id_type=MESH
        )

    ld_new = pltpu.make_async_copy(new_hidden, NH.at[z], lsem.at[0])
    ld_new.start()
    ld_x = pltpu.make_async_copy(store, X, lsem.at[1])
    ld_x.start()

    def block_loads(d):
        rows = pl.ds(pl.multiple_of(rot(z, d) * FEAT, FEAT), FEAT)
        b = d % 2
        return [
            pltpu.make_async_copy(wq.at[rows, :], WQB.at[b], wbsem.at[b, 0]),
            pltpu.make_async_copy(wk.at[rows, :], WKB.at[b], wbsem.at[b, 1]),
            pltpu.make_async_copy(wv.at[rows, :], WVB.at[b], wbsem.at[b, 2]),
        ]

    for d in (0, 1):
        for cp in block_loads(d):
            cp.start()
    own_rows = pl.ds(pl.multiple_of(z * FEAT, FEAT), FEAT)
    ld_w = []
    for h in range(2):
        for kv, ref in enumerate((wk, wv)):
            ld_w.append(
                pltpu.make_async_copy(
                    ref.at[own_rows, h * HD : (h + 1) * HD], W.at[0, h, kv], lsem.at[2 + 2 * h + kv]
                )
            )
    for cp in ld_w:
        cp.start()

    barrier = pltpu.get_barrier_semaphore()
    peers = [zdev[1], zdev[2], zdev[3], xup, xdn, yup, ydn, sib]
    for dev in peers:
        pl.semaphore_signal(barrier, inc=1, device_id=dev, device_id_type=MESH)
    pl.semaphore_wait(barrier, len(peers))

    ring_at = (x, y)

    def seg_rows(cc, k):
        return pl.ds(pl.multiple_of(cc * (4 * SEG) + k * SEG, SEG), SEG)

    def w1_copy(e, h, kv):
        ref = (wk, wv)[kv]
        seg = pl.multiple_of(c * (4 * SEG) + ring_at[kv] * SEG, SEG)
        src = ref.at[pl.ds(pl.multiple_of(rot(z, e) * FEAT + seg, SEG), SEG), h * HD : (h + 1) * HD]
        return rcopy(src, W.at[4 - e, h, kv, pl.ds(seg, SEG), :], w1s.at[kv, h, e], w1r.at[kv, h, 4 - e], zdev[e])

    for kv in range(2):
        for h in range(2):
            for e in (2, 1, 3):
                w1_copy(e, h, kv).start()

    def w1_wait(slot, h, kv):
        seg = pl.multiple_of(c * (4 * SEG) + ring_at[kv] * SEG, SEG)
        dst = W.at[slot, h, kv, pl.ds(seg, SEG), :]
        rcopy(dst, dst, w1s.at[kv, h, slot], w1r.at[kv, h, slot], zdev[slot]).wait_recv()

    lane = lax.broadcasted_iota(jnp.int32, (ROWS, ROWS), 1)
    row = lax.broadcasted_iota(jnp.int32, (ROWS, ROWS), 0)
    eye = lane == row

    def squares_of(v):
        v = v.astype(F32)
        return jnp.sum(v * v, axis=1, keepdims=True)

    ld_new.wait()
    squares = jnp.where(lane == PAGES, squares_of(NH[z]), 0.0)
    ld_x.wait()
    squares = lax.fori_loop(0, PAGES, lambda j, acc: jnp.where(lane == j, squares_of(X[j]), acc), squares)
    SSQ[z] = jnp.transpose(squares)[:16, :]
    for e in (1, 2, 3):
        rcopy(SSQ.at[z], SSQ.at[z], sqs.at[e], sqr.at[e], zdev[e]).start()
    for e in (1, 2, 3):
        far = SSQ.at[rot(z, 4 - e)]
        rcopy(far, far, sqs.at[e], sqr.at[e], zdev[e]).wait_recv()
    total = SSQ[0] + SSQ[1] + SSQ[2] + SSQ[3]
    inverse = lax.rsqrt(total * (1.0 / WIDE) + EPS)
    INV[...] = jnp.transpose(jnp.concatenate([inverse, jnp.zeros((ROWS - 16, ROWS), F32)], axis=0))

    def normed(v, j):
        inv = jnp.sum(jnp.where(lane == j, INV[...], 0.0), axis=1, keepdims=True)
        return (v.astype(F32) * inv * gain[...]).astype(BF16)

    NH[z] = normed(NH[z], PAGES)
    nh_ring = Ring(
        lambda k: NH.at[k], lambda k, s: NH.at[k, pl.ds(64 * s, 64), :], z, zdev[1], zdev[3],
        lambda k: nhs.at[k], lambda k: nhr.at[k],
    )
    nh_ring.start()

    def prepare(j, carry):
        X[j] = normed(X[j], j)
        return carry

    lax.fori_loop(0, PAGES, prepare, 0)

    def w_piece(kv, cc):
        return lambda k: W.at[pl.ds(1, 3), :, kv, seg_rows(cc, k), :]

    def w_half(kv):
        def half(k, s):
            first = pl.multiple_of(c * (4 * SEG) + k * SEG + s * (SEG // 2), SEG // 2)
            return W.at[pl.ds(1, 3), :, kv, pl.ds(first, SEG // 2), :]

        return half

    def w_ring_of(kv, up, down):
        return Ring(
            w_piece(kv, c), w_half(kv), ring_at[kv], up, down, lambda k: w2s.at[kv, k], lambda k: w2r.at[kv, k]
        )

    w_rings = [w_ring_of(0, xup, xdn), w_ring_of(1, yup, ydn)]

    def w3_copy(kv, cc, k, n):
        ref = w_piece(kv, cc)(k)
        return rcopy(ref, ref, w3s.at[kv, n], w3r.at[kv, n], sib)

    for kv in range(2):
        for h in range(2):
            for slot in (1, 2, 3):
                w1_wait(slot, h, kv)
        w_rings[kv].start()
        w3_copy(kv, c, ring_at[kv], 0).start()
    nh_ring.forward_left()
    nh_ring.forward_right()
    for kv in range(2):
        w_rings[kv].forward_left()
        w3_copy(kv, c, w_rings[kv].left, 1).start()
        w_rings[kv].forward_right()
        w3_copy(kv, c, w_rings[kv].right, 2).start()

    sign = jnp.where(lax.broadcasted_iota(jnp.int32, (1, HD), 1) < HD // 2, -1.0, 1.0).astype(F32)
    cos_r, sin_r = cosr[...], sinr[...]

    def angle_at(first_cos, first_sin):
        return first_cos * cos_r - first_sin * sin_r, (first_sin * cos_r + first_cos * sin_r) * sign

    def normed_rope(v, g, cos, sin):
        v = v * lax.rsqrt(jnp.mean(v * v, axis=1, keepdims=True) + EPS) * g
        return (v * cos + pltpu.roll(v, HD // 2, 1) * sin).astype(BF16)

    def project_new(d):
        for cp in block_loads(d):
            cp.wait()
        b = d % 2
        a = NH[rot(z, d)]
        parts = ((0, WQB), (1024, WKB), (1280, WVB))
        for first, ref in parts:
            width = ref.shape[2]
            prod = nn(a, ref[b])
            if d == 0:
                ACC[:, first : first + width] = prod
            else:
                ACC[:, first : first + width] += prod
        if d < 2:
            for cp in block_loads(d + 2):
                cp.start()

    project_new(0)
    project_new(1)
    nh_ring.finish()
    project_new(2)
    project_new(3)
    page_cos, page_sin = cosp[pl.ds(tab[5, 0], 1), :], sinp[pl.ds(tab[5, 0], 1), :]
    rest_cos, rest_sin = cosr[pl.ds(tab[5, 1], 1), :], sinr[pl.ds(tab[5, 1], 1), :]
    cos_new, sin_new = angle_at(
        page_cos * rest_cos - page_sin * rest_sin, page_sin * rest_cos + page_cos * rest_sin
    )
    q_at = (c * 16 + y * 4 + x, c * 16 + x * 4 + y)
    for h in range(2):
        for g in range(GROUP):
            n = h * GROUP + g
            raw = ACC[:, n * HD : (n + 1) * HD]
            QALL[h, q_at[h], g * ROWS : (g + 1) * ROWS, :] = normed_rope(raw, q_gain[...], cos_new, sin_new)

    def q1_ring_of(h):
        base = c * 16 + (y * 4, x * 4)[h]
        up, down = ((xup, xdn), (yup, ydn))[h]
        return Ring(
            lambda k: QALL.at[h, base + k],
            lambda k, s: QALL.at[h, base + k, pl.ds(s * 256, 256), :],
            (x, y)[h], up, down, lambda k: q1s.at[h, k], lambda k: q1r.at[h, k],
        )

    def q2_ring_of(h):
        up, down = ((yup, ydn), (xup, xdn))[h]
        return Ring(
            lambda k: QALL.at[h, pl.ds(c * 16 + k * 4, 4)],
            lambda k, s: QALL.at[h, pl.ds(c * 16 + k * 4 + s * 2, 2)],
            (y, x)[h], up, down, lambda k: q2s.at[h, k], lambda k: q2r.at[h, k],
        )

    q1 = [q1_ring_of(h) for h in range(2)]
    q2 = [q2_ring_of(h) for h in range(2)]

    def q3_copy(h, cc, k, n):
        ref = QALL.at[h, pl.ds(cc * 16 + k * 4, 4)]
        return rcopy(ref, ref, q3s.at[h, n], q3r.at[h, n], sib)

    for h in range(2):
        q1[h].start()

    causal = lax.broadcasted_iota(jnp.int32, (QROWS, ROWS), 1) <= (
        lax.broadcasted_iota(jnp.int32, (QROWS, ROWS), 0) & (ROWS - 1)
    )
    ones = jnp.ones((ROWS, HD), BF16)
    for h in range(2):
        raw = ACC[:, 1024 + h * HD : 1024 + (h + 1) * HD]
        key = normed_rope(raw, k_gain[...], cos_new, sin_new)
        val = (ACC[:, 1280 + h * HD : 1280 + (h + 1) * HD]).astype(BF16)
        scores = nt(QALL[h, q_at[h]], key) * SCALE
        weights = jnp.where(causal, jnp.exp(scores), 0.0).astype(BF16)
        NEWCTX[h] = nn(weights, jnp.concatenate([val, ones], axis=1))

    for kv in range(2):
        w_rings[kv].finish()
        w3_copy(kv, c, w_rings[kv].opp, 3).start()
    for kv in range(2):
        for n, k in enumerate((ring_at[kv], w_rings[kv].left, w_rings[kv].right, w_rings[kv].opp)):
            w3_copy(kv, oc, k, n).wait_recv()
    for cp in ld_w:
        cp.wait()

    def product(i, slot):
        h, pair = i // 6, lax.rem(i, 6)
        a = X[pl.ds(pair * 2, 2)].reshape(2 * ROWS, FEAT)
        return nn(a, jnp.concatenate([W[slot, h, 0], W[slot, h, 1]], axis=1))

    def opp_copy(i, s):
        return rcopy(OPPS.at[i, s], OPPR.at[i, s], os_.at[i, s], or_.at[i, s], (zdev[1], zdev[3])[s])

    def mid_copy(i, s):
        return rcopy(MIDS.at[i, s], MIDR.at[i, s], ms.at[i, s], mr.at[i, s], (zdev[1], zdev[3])[s])

    def opposite(i):
        part = product(i, 2).astype(BF16)
        for s in range(2):
            OPPS[i, s] = part[s * ROWS : (s + 1) * ROWS]
            opp_copy(i, s).start()

    def neighbours(i):
        for s in range(2):
            part = product(i, (1, 3)[s])
            opp_copy(i, s).wait_recv()
            for t in range(2):
                page = part[t * ROWS : (t + 1) * ROWS]
                if t == s:
                    page = page + OPPR[i, s].astype(F32)
                MIDS[i, s, t] = page.astype(BF16)
            mid_copy(i, s).start()

    def own(i):
        h, pair = i // 6, lax.rem(i, 6)
        part = product(i, 0)
        for s in range(2):
            mid_copy(i, s).wait_recv()
        for t in range(2):
            j = pair * 2 + t
            page = part[t * ROWS : (t + 1) * ROWS] + MIDR[i, 0, t].astype(F32) + MIDR[i, 1, t].astype(F32)
            n = h * PAGES + j
            i_page = tab[2, j]
            cos, sin = angle_at(cosp[pl.ds(i_page, 1), :], sinp[pl.ds(i_page, 1), :])
            KB[n] = normed_rope(page[:, :HD], k_gain[...], cos, sin)
            live = row < tab[3, j]
            VB[n, :, :HD] = jnp.where(live, page[:, HD:], 0.0).astype(BF16)
            VB[n, :, HD:] = jnp.where(live, 1.0, 0.0).astype(BF16)

    def attend(n, carry):
        h, j = n // PAGES, lax.rem(n, PAGES)
        scores = nt(QALL[h, tab[h, j]], KB[n]) * SCALE
        mixed = nn(jnp.exp(scores).astype(BF16), VB[n])
        line = lax.broadcasted_iota(jnp.int32, (16, HD), 0)
        for s in range(2):
            CTX[h, j, s, :256, :] = mixed[s * 256 : (s + 1) * 256, :HD].astype(BF16)
            sums = []
            for g in range(2):
                block = mixed[s * 256 + g * ROWS : s * 256 + (g + 1) * ROWS, HD:]
                sums.append(jnp.sum(jnp.where(eye, block, 0.0), axis=0, keepdims=True))
            CTX[h, j, s, 256:, :] = jnp.where(line == 0, sums[0], jnp.where(line == 1, sums[1], 0.0)).astype(BF16)
        return carry

    first_dev = ((xup, xdn), (yup, ydn))
    last_dev = ((yup, ydn), (xup, xdn))
    first_at, last_at = (x, y), (y, x)

    def piece_at(s, a, b):
        return b * 4 + a if s == 0 else a * 4 + b

    def value(h, s, a, b):
        q = piece_at(s, a, b)
        return CTX[h, tab[4, q * 2 + c], s].astype(F32) + R0[h, q, s].astype(F32)

    def c0_copy(h):
        return rcopy(S0, R0.at[h], c0s.at[h], c0r.at[h], sib)

    def c0(h):
        def fill(q, carry):
            S0[q] = CTX[h, tab[4, q * 2 + oc]]
            return carry

        lax.fori_loop(0, 16, fill, 0)
        c0_copy(h).start()

    def c1o_copy(h, s, d):
        part = pl.ds(d * 2, 2)
        return rcopy(S1O.at[h, s, part], R1O.at[h, s, part], c1os.at[h, s, d], c1or.at[h, s, d], first_dev[s][d])

    def c1m_copy(h, s, d):
        return rcopy(S1M.at[h, s, d], R1M.at[h, s, d], c1ms.at[h, s, d], c1mr.at[h, s, d], first_dev[s][d])

    cuts = (pl.ds(0, 128), pl.ds(128, HALF - 128))

    def c2o_copy(h, s, d):
        return rcopy(
            S2O.at[h, s, cuts[d]], R2O.at[h, s, cuts[d]], c2os.at[h, s, d], c2or.at[h, s, d], last_dev[s][d]
        )

    def c2m_copy(h, s, d):
        return rcopy(S2M.at[h, s, d], R2M.at[h, s, d], c2ms.at[h, s, d], c2mr.at[h, s, d], last_dev[s][d])

    def c1(h):
        c0_copy(h).wait_recv()
        for s in range(2):
            a = rot(first_at[s], 2)

            def fill(b, carry):
                S1O[h, s, b] = value(h, s, a, b).astype(BF16)
                return carry

            lax.fori_loop(0, 4, fill, 0)
            for d in range(2):
                c1o_copy(h, s, d).start()

    def c2(h):
        for d in range(2):
            for s in range(2):
                a = rot(first_at[s], (1, 3)[d])
                c1o_copy(h, s, d).wait_recv()

                def with_far(b, carry):
                    S1M[h, s, d, b] = (value(h, s, a, b) + R1O[h, s, b].astype(F32)).astype(BF16)
                    return carry

                def without(b, carry):
                    S1M[h, s, d, b] = value(h, s, a, b).astype(BF16)
                    return carry

                lax.fori_loop(d * 2, d * 2 + 2, with_far, 0)
                lax.fori_loop(2 - d * 2, 4 - d * 2, without, 0)
                c1m_copy(h, s, d).start()

    def c3(h):
        for s in range(2):
            for d in range(2):
                c1m_copy(h, s, d).wait_recv()

            def fill(b, carry):
                A1[s, b] = value(h, s, first_at[s], b) + R1M[h, s, 0, b].astype(F32) + R1M[h, s, 1, b].astype(F32)
                return carry

            lax.fori_loop(0, 4, fill, 0)
            S2O[h, s] = A1[s, rot(last_at[s], 2)].astype(BF16)
            for d in range(2):
                c2o_copy(h, s, d).start()

    def c4(h):
        for s in range(2):
            for d in range(2):
                c2o_copy(h, s, d).wait_recv()
                mine = A1[s, rot(last_at[s], (1, 3)[d])]
                far = R2O[h, s, cuts[d], :].astype(F32)
                if d == 0:
                    total = jnp.concatenate([mine[:128] + far, mine[128:]], axis=0)
                else:
                    total = jnp.concatenate([mine[:128], mine[128:] + far], axis=0)
                S2M[h, s, d] = total.astype(BF16)
                c2m_copy(h, s, d).start()

    def c5(h):
        for s in range(2):
            for d in range(2):
                c2m_copy(h, s, d).wait_recv()
            FIN[...] = A1[s, last_at[s]] + R2M[h, s, 0].astype(F32) + R2M[h, s, 1].astype(F32)
            for g in range(2):
                n = s * 2 + g
                mixed = FIN[g * ROWS : (g + 1) * ROWS, :] + NEWCTX[h, n * ROWS : (n + 1) * ROWS, :HD]
                sums = jnp.sum(jnp.where(eye, FIN[256 + g : 257 + g, :], 0.0), axis=1, keepdims=True)
                sums = sums + NEWCTX[h, n * ROWS : (n + 1) * ROWS, HD:]
                m = h * GROUP + n
                out[:, m * HD : (m + 1) * HD] = (mixed / sums).astype(BF16)

    CTX[0, PAGES] = jnp.zeros((2, HALF, HD), BF16)
    CTX[1, PAGES] = jnp.zeros((2, HALF, HD), BF16)

    def step(i, carry):
        @pl.when(i < ITEMS)
        def _():
            opposite(i)

        @pl.when(jnp.logical_and(i >= 1, i <= ITEMS))
        def _():
            neighbours(i - 1)

        @pl.when(i >= 2)
        def _():
            own(i - 2)

        @pl.when(i == 1)
        def _():
            for h in range(2):
                q1[h].forward_left()
                q1[h].forward_right()

        @pl.when(i == 2)
        def _():
            for h in range(2):
                q1[h].finish()
                q2[h].start()
                q3_copy(h, c, (y, x)[h], 0).start()

        @pl.when(i == 5)
        def _():
            for h in range(2):
                q2[h].forward_left()
                q3_copy(h, c, q2[h].left, 1).start()
                q2[h].forward_right()
                q3_copy(h, c, q2[h].right, 2).start()

        @pl.when(i == 6)
        def _():
            for h in range(2):
                q2[h].finish()
                q3_copy(h, c, q2[h].opp, 3).start()

        @pl.when(i == 7)
        def _():
            for h in range(2):
                for n, k in enumerate((q2[h].at, q2[h].left, q2[h].right, q2[h].opp)):
                    q3_copy(h, oc, k, n).wait_recv()
            lax.fori_loop(0, PAGES, attend, 0)
            c0(0)

        @pl.when(i >= 8)
        def _():
            lax.fori_loop(2 * (i - 2), 2 * (i - 1), attend, 0)

        for k, stage in ((8, c1), (9, c2), (10, c3), (11, c4), (12, c5)):

            @pl.when(i == k)
            def _(stage=stage):
                stage(0)

        return carry

    lax.fori_loop(0, ITEMS + 2, step, 0)
    c0_copy(0).wait_send()
    for stage in (c0, c1, c2, c3, c4, c5):
        stage(1)

    c0_copy(1).wait_send()
    for kv in range(2):
        for h in range(2):
            for e in (1, 2, 3):
                w1_copy(e, h, kv).wait_send()
        w_rings[kv].drain()
        for n, k in enumerate((ring_at[kv], w_rings[kv].left, w_rings[kv].right, w_rings[kv].opp)):
            w3_copy(kv, c, k, n).wait_send()
    nh_ring.drain()
    for e in (1, 2, 3):
        rcopy(SSQ.at[z], SSQ.at[z], sqs.at[e], sqr.at[e], zdev[e]).wait_send()

    def drain(i, carry):
        for s in range(2):
            opp_copy(i, s).wait_send()
            mid_copy(i, s).wait_send()
        return carry

    lax.fori_loop(0, ITEMS, drain, 0)
    for h in range(2):
        q1[h].drain()
        q2[h].drain()
        for n, k in enumerate((q2[h].at, q2[h].left, q2[h].right, q2[h].opp)):
            q3_copy(h, c, k, n).wait_send()
        for s in range(2):
            for d in range(2):
                c1o_copy(h, s, d).wait_send()
                c1m_copy(h, s, d).wait_send()
                c2o_copy(h, s, d).wait_send()
                c2m_copy(h, s, d).wait_send()


def local(store, new_hidden, wq, wk, wv, norm_gain, q_gain, k_gain, page_table, hist_len):
    p = lax.axis_index("pool")
    z = lax.axis_index("tensor")
    flat = page_table.reshape(1, -1)
    entry = jnp.arange(flat.shape[1], dtype=jnp.int32)[None, :]
    request, place = entry // 16, entry % 16
    room = jnp.clip(jnp.repeat(hist_len, 16)[None, :] - place * ROWS, 0, ROWS)
    listed = flat == p * PAGES + jnp.arange(32, dtype=jnp.int32)[:, None]
    listed = jnp.logical_and(listed, jnp.arange(32, dtype=jnp.int32)[:, None] < PAGES)

    def pick(v):
        return jnp.sum(jnp.where(listed, v, 0), axis=1)

    page_request = pick(request)
    core, xx, yy = page_request % 2, (page_request // 2) % 4, page_request // 8
    mine = jnp.logical_and(page_table >= 0, page_table // PAGES == p)
    slot = PAGES + jnp.sum(jnp.where(mine, page_table % PAGES - PAGES, 0), axis=1)
    length = jnp.broadcast_to(lax.dynamic_index_in_dim(hist_len, p, 0, keepdims=False), (32,))
    first = jnp.arange(32) == 0
    tab = jnp.stack(
        [
            core * 16 + yy * 4 + xx,
            core * 16 + xx * 4 + yy,
            pick(place),
            pick(room),
            slot,
            jnp.where(first, length // ROWS, length % ROWS),
        ]
    ).astype(jnp.int32)
    gain = lax.dynamic_slice_in_dim(norm_gain, z * FEAT, FEAT, 0).reshape(1, FEAT)
    tables = [jnp.asarray(t) for t in rope_tables()]
    vm = pl.BlockSpec(memory_space=pltpu.VMEM)
    hbm = pl.BlockSpec(memory_space=pl.ANY)
    dma = pltpu.SemaphoreType.DMA
    scratch = [
        pltpu.VMEM((PAGES, ROWS, FEAT), BF16),
        pltpu.VMEM((4, 2, 2, FEAT, HD), BF16),
        pltpu.VMEM((2, FEAT, 1024), BF16),
        pltpu.VMEM((2, FEAT, 256), BF16),
        pltpu.VMEM((2, FEAT, 256), BF16),
        pltpu.VMEM((ROWS, 1536), F32),
        pltpu.VMEM((4, ROWS, FEAT), BF16),
        pltpu.VMEM((4, 16, ROWS), F32),
        pltpu.VMEM((ROWS, ROWS), F32),
        pltpu.VMEM((ITEMS, 2, ROWS, 256), BF16),
        pltpu.VMEM((ITEMS, 2, ROWS, 256), BF16),
        pltpu.VMEM((ITEMS, 2, 2, ROWS, 256), BF16),
        pltpu.VMEM((ITEMS, 2, 2, ROWS, 256), BF16),
        pltpu.VMEM((2 * PAGES, ROWS, HD), BF16),
        pltpu.VMEM((2 * PAGES, ROWS, 2 * HD), BF16),
        pltpu.VMEM((2, QROWS, 2 * HD), F32),
        pltpu.VMEM((2, REQS, QROWS, HD), BF16),
        pltpu.VMEM((2, PAGES + 1, 2, HALF, HD), BF16),
        pltpu.VMEM((16, 2, HALF, HD), BF16),
        pltpu.VMEM((2, 16, 2, HALF, HD), BF16),
        pltpu.VMEM((2, 2, 4, HALF, HD), BF16),
        pltpu.VMEM((2, 2, 4, HALF, HD), BF16),
        pltpu.VMEM((2, 2, 2, 4, HALF, HD), BF16),
        pltpu.VMEM((2, 2, 2, 4, HALF, HD), BF16),
        pltpu.VMEM((2, 4, HALF, HD), F32),
        pltpu.VMEM((2, 2, HALF, HD), BF16),
        pltpu.VMEM((2, 2, HALF, HD), BF16),
        pltpu.VMEM((2, 2, 2, HALF, HD), BF16),
        pltpu.VMEM((2, 2, 2, HALF, HD), BF16),
        pltpu.VMEM((HALF, HD), F32),
        dma((6,)), dma((2, 3)),
        dma((2, 2, 4)), dma((2, 2, 4)), dma((2, 4)), dma((2, 4)), dma((2, 4)), dma((2, 4)),
        dma((4,)), dma((4,)), dma((4,)), dma((4,)),
        dma((ITEMS, 2)), dma((ITEMS, 2)), dma((ITEMS, 2)), dma((ITEMS, 2)),
        dma((2, 4)), dma((2, 4)), dma((2, 4)), dma((2, 4)), dma((2, 4)), dma((2, 4)),
        dma((2,)), dma((2,)),
        dma((2, 2, 2)), dma((2, 2, 2)), dma((2, 2, 2)), dma((2, 2, 2)),
        dma((2, 2, 2)), dma((2, 2, 2)), dma((2, 2, 2)), dma((2, 2, 2)),
    ]
    return pl.pallas_call(
        kernel,
        out_shape=jax.ShapeDtypeStruct((ROWS, 2 * GROUP * HD), BF16),
        in_specs=[pl.BlockSpec(memory_space=pltpu.SMEM)] + [hbm] * 5 + [vm] * 7,
        out_specs=vm,
        scratch_shapes=scratch,
        compiler_params=pltpu.CompilerParams(
            collective_id=0, has_side_effects=True, vmem_limit_bytes=63 * 1024 * 1024
        ),
        cost_estimate=pl.CostEstimate(flops=12_000_000_000, bytes_accessed=25_000_000, transcendentals=2_000_000),
    )(tab, store, new_hidden, wq, wk, wv, gain, q_gain.reshape(1, HD), k_gain.reshape(1, HD), *tables)


def solution(mesh):
    return jax.shard_map(
        local,
        mesh=mesh,
        in_specs=(
            P("pool", None, "tensor"),
            P("pool", "tensor"),
            P(None, "tensor"),
            P(None, "tensor"),
            P(None, "tensor"),
            P(),
            P(),
            P(),
            P(),
            P(),
        ),
        out_specs=P("pool", "tensor"),
        check_vma=False,
    )
```

time: 436 us -> 142 us (0.33)
  waiting for transfers between devices: 285 us -> 0 us
  Pallas kernels: 0 us -> 130 us
  other arithmetic: 62.5 us -> 1.02 us
  matrix products: 34 us -> 0 us
  local copies, waits for them, and re-layouts: 30.4 us -> 6.57 us
  between operations: 13.8 us -> 2.66 us
  starting transfers between devices: 8.89 us -> 0 us
    all_gather x2 -> x0, waiting for transfers between devices: 160 us -> none  [the longest x1 160 us: local(): whole_hist = lax.all_gather(ordered, 'tensor', axis=2, tiled=True)]
    pallas_call x0 -> x1, Pallas kernels: none -> 130 us  [local(): pl.pallas_call(kernel, out_shape=jax.ShapeDtypeStruct((ROWS, 2 * GROUP *...]
    all_to_all x1 -> x0, waiting for transfers between devices: 125 us -> none  [local(): lax.all_to_all(outgoing, 'pool', split_axis=0, concat_axis=0, tiled=True)]
    dot_general x7 -> x0, matrix products: 34 us -> none  [the longest x1 11 us: project_pages(): jnp.dot(normed, wv, preferred_element_type=jnp.float32).astype(jnp.bfloat16)]
    convert_element_type x4 -> x0, other arithmetic: 23.6 us -> none  [the longest x2 22.9 us: rms_rows(): return (values * inv_rms * gain_vec).astype(jnp.bfloat16)]
    select_n x4 -> x2, other arithmetic: 17.5 us -> 0.01 us  [the longest x1 0.01 us: local(): jnp.where(first, length // ROWS, length % ROWS)]
    gather x2 -> x0, local copies, waits for them, and re-layouts: 15 us -> none  [the longest x1 7.8 us: local(): chosen = jnp.take(store, send_slot, axis=0)]
    reduce_sum x4 -> x2, other arithmetic: 12.7 us -> 0.96 us  [the longest x1 0.73 us: local(): jnp.sum(jnp.where(mine, page_table % PAGES - PAGES, 0), axis=1)]
  transfers between devices with their start and end apart: 3 -> 0, of which waited for: 2 -> 0; matrix products, arithmetic and copies ran while one was open for 11% -> 0% of each run, Pallas kernels for 0% -> 0%
where the time goes in v1:
time: 142 us; the launch traced here: 141 us
  Pallas kernels  130 us (92%)
  local copies, waits for them, and re-layouts  6.57 us (5%)
  between operations  2.66 us (2%)
    pallas_call x1, Pallas kernels, local(): pl.pallas_call(kernel, out_shape=jax.ShapeDtypeStruct((ROWS, 2 * GROUP *...  130 us

profile of v1, /device:TPU:1, one launch (start us, length us, event | category | flops | bytes accessed | tf_op | source)
XLA Modules:
  0.0 140.7 jit_solution(9032763038713686219)
XLA Ops:
  0.0 1.2 dynamic_slice.7
  3.9 0.7 fusion.3
  4.6 0.8 dynamic_slice.8
  5.4 0.6 reshape.260.gain
  6.0 0.8 copy.16
  6.8 0.1 eq.40
  6.9 0.7 broadcast_in_dim.40
  7.6 0.1 broadcast_in_dim_reshape.3
  7.7 0.2 select_reduce_fusion
  8.0 0.6 stack.15.tab
  8.6 130.4 %shard_map.136 = bf16[128,1024]{1,0:T(8,128)(2,1)} custom-call(s32[6,32]{1,0:T(8,128)} %stack.15.tab, bf16[12,128,1280]{2,1,0:T(8,128)(2,1)} %store.1, bf16[128,1280]{1,0:T(8,128)(2,1)} %new_hidden.1, bf16[5120,1024]{1,0:T(8,128)(2,1)} %wq.1, bf16[5120,256]{1,0:T(8,128)(2,1)} %wk.1, bf16[5120,256]{1,0:T(8,128)(2,1)} %wv.1, f32[1,1280]{1,0:T(1,128)} %reshape.260.gain, ...), custom_call_target="tpu_custom_call" | custom-call | flops 12000000000 | bytes 25000000 | tf_op jit(solution)/shard_map/pallas_call | solution.py:677
  139.0 1.7 %copy.18 = bf16[128,1024]{1,0:T(8,128)(2,1)} copy(bf16[128,1024]{1,0:T(8,128)(2,1)} %shard_map.136) | data formatting | bytes 524288
  (7 shorter events, 0.1 us)

commit v2 on v1

v2 whole, which is shorter than its diff:
```python
import jax
import jax.numpy as jnp
import numpy as np
from jax import lax
from jax.experimental import pallas as pl
from jax.experimental.pallas import tpu as pltpu
from jax.sharding import PartitionSpec as P

EPS = 1e-06
ROPE_BASE = 1000000.0
MESH = pl.DeviceIdType.MESH
F32 = jnp.float32
BF16 = jnp.bfloat16

PAGES = 12
ROWS = 128
FEAT = 1280
NZ = 4
WIDE = FEAT * NZ
HD = 128
GROUP = 4
QROWS = GROUP * ROWS
REQS = 32
ITEMS = 12
HALF = 272
SEG = 160
SCALE = HD ** -0.5


def rope_tables():
    freq = ROPE_BASE ** (-np.arange(64, dtype=np.float64) * 2.0 / HD)
    freq = np.concatenate([freq, freq])[None, :]
    rows = np.arange(ROWS, dtype=np.float64)[:, None] * freq
    pages = np.arange(24, dtype=np.float64)[:, None] * ROWS * freq
    return [np.asarray(t, np.float32) for t in (np.cos(rows), np.sin(rows), np.cos(pages), np.sin(pages))]


class Ring:
    def __init__(self, piece, half, at, dev_up, dev_down, send, recv):
        self.piece, self.half, self.at = piece, half, at
        self.up, self.down, self.send, self.recv = dev_up, dev_down, send, recv
        self.left = lax.rem(at + 3, 4)
        self.right = lax.rem(at + 1, 4)
        self.opp = lax.rem(at + 2, 4)

    def copy(self, ref, k, dev):
        return pltpu.make_async_remote_copy(
            src_ref=ref, dst_ref=ref, send_sem=self.send(k), recv_sem=self.recv(k), device_id=dev, device_id_type=MESH
        )

    def start(self):
        self.copy(self.piece(self.at), 0, self.up).start()
        self.copy(self.piece(self.at), 1, self.down).start()

    def forward_left(self):
        self.copy(self.piece(self.left), 0, self.up).wait_recv()
        self.copy(self.half(self.left, 0), 2, self.up).start()

    def forward_right(self):
        self.copy(self.piece(self.right), 1, self.down).wait_recv()
        self.copy(self.half(self.right, 1), 3, self.down).start()

    def finish(self):
        self.copy(self.half(self.opp, 0), 2, self.up).wait_recv()
        self.copy(self.half(self.opp, 1), 3, self.down).wait_recv()

    def drain(self):
        self.copy(self.piece(self.at), 0, self.up).wait_send()
        self.copy(self.piece(self.at), 1, self.down).wait_send()
        self.copy(self.half(self.left, 0), 2, self.up).wait_send()
        self.copy(self.half(self.right, 1), 3, self.down).wait_send()


def nt(a, b):
    return lax.dot_general(a, b, (((1,), (1,)), ((), ())), preferred_element_type=F32)


def nn(a, b):
    return jnp.dot(a, b, preferred_element_type=F32)


def kernel(
    table, lengths, store, new_hidden, wq, wk, wv, norm_gain, q_gain, k_gain, cosr, sinr, cosp, sinp,
    out,
    X, W, WQB, WKB, WVB, ACC, NH, SSQ, INV, OPPS, OPPR, MIDS, MIDR, KB, VB, NEWCTX, QA, QB, CTX,
    S0, R0, S1O, R1O, S1M, R1M, A1, S2O, R2O, S2M, R2M, FIN, TV, TS,
    lsem, wbsem, w1s, w1r, w2s, w2r, w3s, w3r, nhs, nhr, sqs, sqr, os_, or_, ms, mr,
    q1s, q1r, q2s, q2r, q3s, q3r, c0s, c0r, c1os, c1or, c1ms, c1mr, c2os, c2or, c2ms, c2mr,
):
    QS = (QA, QB)
    p = lax.axis_index("pool")
    z = lax.axis_index("tensor")
    c = lax.rem(p, 2)
    x = lax.rem(p // 2, 4)
    y = p // 8
    oc = 1 - c

    def at(yy, xx, cc):
        return yy * 8 + xx * 2 + cc

    def rot(v, d):
        return lax.rem(v + d, 4)

    zdev = [(p, rot(z, d)) for d in range(4)]
    xup, xdn = (at(y, rot(x, 1), c), z), (at(y, rot(x, 3), c), z)
    yup, ydn = (at(rot(y, 1), x, c), z), (at(rot(y, 3), x, c), z)
    sib = (at(y, x, oc), z)

    def rcopy(src, dst, ss, rs, dev):
        return pltpu.make_async_remote_copy(
            src_ref=src, dst_ref=dst, send_sem=ss, recv_sem=rs, device_id=dev, device_id_type=MESH
        )

    ld_new = pltpu.make_async_copy(new_hidden, NH.at[z], lsem.at[0])
    ld_new.start()
    ld_x = [pltpu.make_async_copy(store.at[pl.ds(6 * n, 6)], X.at[pl.ds(6 * n, 6)], lsem.at[1 + n]) for n in range(2)]
    for cp in ld_x:
        cp.start()

    barrier = pltpu.get_barrier_semaphore()
    peers = [zdev[1], zdev[2], zdev[3], xup, xdn, yup, ydn, sib]
    for dev in peers:
        pl.semaphore_signal(barrier, inc=1, device_id=dev, device_id_type=MESH)

    page = table[...] - p * PAGES
    hit = jnp.logical_and(page >= 0, page < PAGES)
    rank = lax.broadcasted_iota(jnp.int32, (16, REQS), 0)
    slots = PAGES + jnp.sum(jnp.where(hit, page - PAGES, 0), axis=0, keepdims=True)
    askers = jnp.where(slots == rank, lax.broadcasted_iota(jnp.int32, (16, REQS), 1), 0)
    TV[...] = jnp.zeros_like(TV)
    TV[0:1, :REQS] = jnp.clip(slots, 0, PAGES)
    TV[1:2, :REQS] = jnp.clip(jnp.sum(jnp.where(hit, rank, 0), axis=0, keepdims=True), 0, 15)
    TV[8:24, :] = jnp.broadcast_to(jnp.clip(jnp.sum(askers, axis=1, keepdims=True), 0, REQS - 1), (16, HD))
    to_scalar = pltpu.make_async_copy(TV, TS, lsem.at[3])
    to_scalar.start()

    CTX[0, PAGES] = jnp.zeros((2, HALF, HD), BF16)
    CTX[1, PAGES] = jnp.zeros((2, HALF, HD), BF16)

    lane = lax.broadcasted_iota(jnp.int32, (ROWS, ROWS), 1)
    row = lax.broadcasted_iota(jnp.int32, (ROWS, ROWS), 0)
    eye = lane == row
    gain = jnp.concatenate([norm_gain[pl.ds(z * (FEAT // HD) + k, 1), :] for k in range(FEAT // HD)], axis=1)

    def squares_of(v):
        v = v.astype(F32)
        return jnp.sum(v * v, axis=1, keepdims=True)

    ld_new.wait()
    squares = jnp.where(lane == PAGES, squares_of(NH[z]), 0.0)
    for n in range(2):
        ld_x[n].wait()
        squares = lax.fori_loop(
            6 * n, 6 * n + 6, lambda j, acc: jnp.where(lane == j, squares_of(X[j]), acc), squares
        )
    SSQ[z] = jnp.transpose(squares)[:16, :]
    to_scalar.wait()

    def block_loads(d):
        rows = pl.ds(pl.multiple_of(rot(z, d) * FEAT, FEAT), FEAT)
        b = (0, 1, 1, 0)[d]
        return [
            pltpu.make_async_copy(wq.at[rows, :], WQB.at[b], wbsem.at[b, 0]),
            pltpu.make_async_copy(wk.at[rows, :], WKB.at[b], wbsem.at[b, 1]),
            pltpu.make_async_copy(wv.at[rows, :], WVB.at[b], wbsem.at[b, 2]),
        ]

    own_rows = pl.ds(pl.multiple_of(z * FEAT, FEAT), FEAT)
    ld_w = []
    for h in range(2):
        for kv, ref in enumerate((wk, wv)):
            ld_w.append(
                pltpu.make_async_copy(
                    ref.at[own_rows, h * HD : (h + 1) * HD], W.at[0, h, kv], lsem.at[4 + 2 * h + kv]
                )
            )

    pl.semaphore_wait(barrier, len(peers))
    for e in (1, 2, 3):
        rcopy(SSQ.at[z], SSQ.at[z], sqs.at[e], sqr.at[e], zdev[e]).start()

    ring_at = (x, y)

    def seg_rows(cc, k):
        return pl.ds(pl.multiple_of(cc * (4 * SEG) + k * SEG, SEG), SEG)

    def w1_copy(e, h, kv):
        ref = (wk, wv)[kv]
        seg = pl.multiple_of(c * (4 * SEG) + ring_at[kv] * SEG, SEG)
        src = ref.at[pl.ds(pl.multiple_of(rot(z, e) * FEAT + seg, SEG), SEG), h * HD : (h + 1) * HD]
        return rcopy(src, W.at[4 - e, h, kv, pl.ds(seg, SEG), :], w1s.at[kv, h, e], w1r.at[kv, h, 4 - e], zdev[e])

    for h in range(2):
        for kv in range(2):
            for e in (2, 1, 3):
                w1_copy(e, h, kv).start()

    def w1_wait(slot, h, kv):
        seg = pl.multiple_of(c * (4 * SEG) + ring_at[kv] * SEG, SEG)
        dst = W.at[slot, h, kv, pl.ds(seg, SEG), :]
        rcopy(dst, dst, w1s.at[kv, h, slot], w1r.at[kv, h, slot], zdev[slot]).wait_recv()

    for d in (0, 1):
        for cp in block_loads(d):
            cp.start()
    for cp in ld_w:
        cp.start()

    for e in (1, 2, 3):
        far = SSQ.at[rot(z, 4 - e)]
        rcopy(far, far, sqs.at[e], sqr.at[e], zdev[e]).wait_recv()
    total = SSQ[0] + SSQ[1] + SSQ[2] + SSQ[3]
    inverse = lax.rsqrt(total * (1.0 / WIDE) + EPS)
    INV[...] = jnp.transpose(jnp.concatenate([inverse, jnp.zeros((ROWS - 16, ROWS), F32)], axis=0))

    def normed(v, j):
        inv = jnp.sum(jnp.where(lane == j, INV[...], 0.0), axis=1, keepdims=True)
        return (v.astype(F32) * inv * gain).astype(BF16)

    NH[z] = normed(NH[z], PAGES)
    nh_ring = Ring(
        lambda k: NH.at[k], lambda k, s: NH.at[k, pl.ds(64 * s, 64), :], z, zdev[1], zdev[3],
        lambda k: nhs.at[k], lambda k: nhr.at[k],
    )
    nh_ring.start()

    def prepare(j, carry):
        X[j] = normed(X[j], j)
        return carry

    lax.fori_loop(0, PAGES, prepare, 0)

    def w_piece(h, kv, cc):
        return lambda k: W.at[pl.ds(1, 3), h, kv, seg_rows(cc, k), :]

    def w_half(h, kv):
        def half(k, s):
            first = pl.multiple_of(c * (4 * SEG) + k * SEG + s * (SEG // 2), SEG // 2)
            return W.at[pl.ds(1, 3), h, kv, pl.ds(first, SEG // 2), :]

        return half

    def w_ring_of(h, kv):
        up, down = ((xup, xdn), (yup, ydn))[kv]
        return Ring(
            w_piece(h, kv, c), w_half(h, kv), ring_at[kv], up, down,
            lambda k: w2s.at[h, kv, k], lambda k: w2r.at[h, kv, k],
        )

    w_rings = [[w_ring_of(h, kv) for kv in range(2)] for h in range(2)]

    def w3_copy(h, kv, cc, n):
        ring = w_rings[h][kv]
        ref = w_piece(h, kv, cc)((ring.at, ring.left, ring.right, ring.opp)[n])
        return rcopy(ref, ref, w3s.at[h, kv, n], w3r.at[h, kv, n], sib)

    def w_start(h):
        for kv in range(2):
            for slot in (1, 2, 3):
                w1_wait(slot, h, kv)
            w_rings[h][kv].start()
            w3_copy(h, kv, c, 0).start()

    def w_forward(h):
        for kv in range(2):
            w_rings[h][kv].forward_left()
            w3_copy(h, kv, c, 1).start()
            w_rings[h][kv].forward_right()
            w3_copy(h, kv, c, 2).start()

    def w_finish(h):
        for kv in range(2):
            w_rings[h][kv].finish()
            w3_copy(h, kv, c, 3).start()

    def w_wait(h):
        for kv in range(2):
            for n in range(4):
                w3_copy(h, kv, oc, n).wait_recv()
            ld_w[2 * h + kv].wait()

    sign = jnp.where(lax.broadcasted_iota(jnp.int32, (1, HD), 1) < HD // 2, -1.0, 1.0).astype(F32)
    cos_r, sin_r = cosr[...], sinr[...]

    def angle_at(first_cos, first_sin):
        return first_cos * cos_r - first_sin * sin_r, (first_sin * cos_r + first_cos * sin_r) * sign

    def normed_rope(v, g, cos, sin):
        v = v * lax.rsqrt(jnp.mean(v * v, axis=1, keepdims=True) + EPS) * g
        return (v * cos + pltpu.roll(v, HD // 2, 1) * sin).astype(BF16)

    def project_new(d):
        for cp in block_loads(d):
            cp.wait()
        b = (0, 1, 1, 0)[d]
        a = NH[rot(z, d)]
        parts = ((0, WQB), (1024, WKB), (1280, WVB))
        for first, ref in parts:
            width = ref.shape[2]
            prod = nn(a, ref[b])
            if d == 0:
                ACC[:, first : first + width] = prod
            else:
                ACC[:, first : first + width] += prod
        if d < 2:
            for cp in block_loads(3 - d):
                cp.start()

    w_start(0)
    project_new(0)
    w_start(1)
    w_forward(0)
    nh_ring.forward_left()
    nh_ring.forward_right()
    project_new(1)
    project_new(3)
    w_finish(0)
    w_forward(1)
    w_wait(0)

    def product(i, slot):
        h, pair = i // 6, lax.rem(i, 6)
        a = X[pl.ds(pair * 2, 2)].reshape(2 * ROWS, FEAT)
        return nn(a, jnp.concatenate([W[slot, h, 0], W[slot, h, 1]], axis=1))

    def opp_copy(i, s):
        return rcopy(OPPS.at[i, s], OPPR.at[i, s], os_.at[i, s], or_.at[i, s], (zdev[1], zdev[3])[s])

    def mid_copy(i, s):
        return rcopy(MIDS.at[i, s], MIDR.at[i, s], ms.at[i, s], mr.at[i, s], (zdev[1], zdev[3])[s])

    def opposite(i):
        part = product(i, 2).astype(BF16)
        for s in range(2):
            OPPS[i, s] = part[s * ROWS : (s + 1) * ROWS]
            opp_copy(i, s).start()

    def neighbours(i):
        for s in range(2):
            part = product(i, (1, 3)[s])
            opp_copy(i, s).wait_recv()
            for t in range(2):
                page = part[t * ROWS : (t + 1) * ROWS]
                if t == s:
                    page = page + OPPR[i, s].astype(F32)
                MIDS[i, s, t] = page.astype(BF16)
            mid_copy(i, s).start()

    def own(i):
        h, pair = i // 6, lax.rem(i, 6)
        part = product(i, 0)
        for s in range(2):
            mid_copy(i, s).wait_recv()
        for t in range(2):
            j = pair * 2 + t
            page = part[t * ROWS : (t + 1) * ROWS] + MIDR[i, 0, t].astype(F32) + MIDR[i, 1, t].astype(F32)
            n = h * PAGES + j
            request = TS[8 + j, 0]
            i_page = TS[1, request]
            cos, sin = angle_at(cosp[pl.ds(i_page, 1), :], sinp[pl.ds(i_page, 1), :])
            KB[n] = normed_rope(page[:, :HD], k_gain[...], cos, sin)
            live = row < lengths[request] - i_page * ROWS
            VB[n, :, :HD] = jnp.where(live, page[:, HD:], 0.0).astype(BF16)
            VB[n, :, HD:] = jnp.where(live, 1.0, 0.0).astype(BF16)

    def attend(h, j):
        n = h * PAGES + j
        request = TS[8 + j, 0]
        core, xx, yy = lax.rem(request, 2), lax.rem(request // 2, 4), request // 8
        query = jnp.concatenate(
            [QS[h][0, core * 16 + yy * 4 + xx], QS[h][1, core * 16 + xx * 4 + yy]], axis=0
        )
        scores = nt(query, KB[n]) * SCALE
        mixed = nn(jnp.exp(scores).astype(BF16), VB[n])
        line = lax.broadcasted_iota(jnp.int32, (16, HD), 0)
        for s in range(2):
            CTX[h, j, s, :256, :] = mixed[s * 256 : (s + 1) * 256, :HD].astype(BF16)
            sums = []
            for g in range(2):
                block = mixed[s * 256 + g * ROWS : s * 256 + (g + 1) * ROWS, HD:]
                sums.append(jnp.sum(jnp.where(eye, block, 0.0), axis=0, keepdims=True))
            CTX[h, j, s, 256:, :] = jnp.where(line == 0, sums[0], jnp.where(line == 1, sums[1], 0.0)).astype(BF16)

    def attend_pages(h, first, last):
        def one(j, carry):
            attend(h, j)
            return carry

        lax.fori_loop(first, last, one, 0)

    opposite(0)
    opposite(1)
    w_finish(1)
    nh_ring.finish()
    project_new(2)
    length = lengths[p]
    page_cos, page_sin = cosp[pl.ds(length // ROWS, 1), :], sinp[pl.ds(length // ROWS, 1), :]
    rest_cos, rest_sin = cosr[pl.ds(lax.rem(length, ROWS), 1), :], sinr[pl.ds(lax.rem(length, ROWS), 1), :]
    cos_new, sin_new = angle_at(
        page_cos * rest_cos - page_sin * rest_sin, page_sin * rest_cos + page_cos * rest_sin
    )

    q_at = (c * 16 + y * 4 + x, c * 16 + x * 4 + y)

    def q1_ring_of(h, s):
        base = c * 16 + (y * 4, x * 4)[s]
        up, down = ((xup, xdn), (yup, ydn))[s]
        return Ring(
            lambda k: QS[h].at[s, base + k],
            lambda k, t: QS[h].at[s, base + k, pl.ds(t * 128, 128), :],
            (x, y)[s], up, down, lambda k: q1s.at[h, s, k], lambda k: q1r.at[h, s, k],
        )

    def q2_ring_of(h, s):
        up, down = ((yup, ydn), (xup, xdn))[s]
        return Ring(
            lambda k: QS[h].at[s, pl.ds(c * 16 + k * 4, 4)],
            lambda k, t: QS[h].at[s, pl.ds(c * 16 + k * 4 + t * 2, 2)],
            (y, x)[s], up, down, lambda k: q2s.at[h, s, k], lambda k: q2r.at[h, s, k],
        )

    q1 = [[q1_ring_of(h, s) for s in range(2)] for h in range(2)]
    q2 = [[q2_ring_of(h, s) for s in range(2)] for h in range(2)]

    def q3_copy(h, s, cc, n):
        k = (q2[h][s].at, q2[h][s].left, q2[h][s].right, q2[h][s].opp)[n]
        ref = QS[h].at[s, pl.ds(cc * 16 + k * 4, 4)]
        return rcopy(ref, ref, q3s.at[h, s, n], q3r.at[h, s, n], sib)

    for h in range(2):
        for s in range(2):
            for g in range(2):
                n = h * GROUP + s * 2 + g
                raw = ACC[:, n * HD : (n + 1) * HD]
                QS[h][s, q_at[s], g * ROWS : (g + 1) * ROWS, :] = normed_rope(raw, q_gain[...], cos_new, sin_new)
            q1[h][s].start()

    def q1_forward(h):
        for s in range(2):
            q1[h][s].forward_left()
            q1[h][s].forward_right()

    def q2_start(h):
        for s in range(2):
            q1[h][s].finish()
            q2[h][s].start()
            q3_copy(h, s, c, 0).start()

    def q2_forward(h):
        for s in range(2):
            q2[h][s].forward_left()
            q3_copy(h, s, c, 1).start()
            q2[h][s].forward_right()
            q3_copy(h, s, c, 2).start()

    def q2_finish(h):
        for s in range(2):
            q2[h][s].finish()
            q3_copy(h, s, c, 3).start()

    def q3_wait(h):
        for s in range(2):
            for n in range(4):
                q3_copy(h, s, oc, n).wait_recv()

    def attend_new():
        causal = lax.broadcasted_iota(jnp.int32, (QROWS, ROWS), 1) <= (
            lax.broadcasted_iota(jnp.int32, (QROWS, ROWS), 0) & (ROWS - 1)
        )
        ones = jnp.ones((ROWS, HD), BF16)
        for h in range(2):
            key = normed_rope(ACC[:, 1024 + h * HD : 1024 + (h + 1) * HD], k_gain[...], cos_new, sin_new)
            val = ACC[:, 1280 + h * HD : 1280 + (h + 1) * HD].astype(BF16)
            query = jnp.concatenate([QS[h][0, q_at[0]], QS[h][1, q_at[1]]], axis=0)
            scores = nt(query, key) * SCALE
            weights = jnp.where(causal, jnp.exp(scores), 0.0).astype(BF16)
            NEWCTX[h] = nn(weights, jnp.concatenate([val, ones], axis=1))

    first_dev = ((xup, xdn), (yup, ydn))
    last_dev = ((yup, ydn), (xup, xdn))
    first_at, last_at = (x, y), (y, x)

    def mine(h, s, o, b, core):
        a = rot(first_at[s], o)
        chip = b * 4 + a if s == 0 else a * 4 + b
        return CTX[h, TS[0, chip * 2 + core], s]

    def value(h, s, o, b):
        return mine(h, s, o, b, c).astype(F32) + R0[h, s, o, b].astype(F32)

    def c0_copy(h, s, o):
        return rcopy(S0.at[s, o], R0.at[h, s, o], c0s.at[h, s, o], c0r.at[h, s, o], sib)

    def c0(h):
        for o in (2, 1, 3, 0):
            for s in range(2):

                def fill(b, carry):
                    S0[s, o, b] = mine(h, s, o, b, oc)
                    return carry

                lax.fori_loop(0, 4, fill, 0)
                c0_copy(h, s, o).start()

    def c1o_copy(h, s, d):
        part = pl.ds(d * 2, 2)
        return rcopy(S1O.at[h, s, part], R1O.at[h, s, part], c1os.at[h, s, d], c1or.at[h, s, d], first_dev[s][d])

    def c1m_copy(h, s, d, n):
        part = pl.ds(n * 2, 2)
        return rcopy(
            S1M.at[h, s, d, part], R1M.at[h, s, d, part], c1ms.at[h, s, d, n], c1mr.at[h, s, d, n], first_dev[s][d]
        )

    cuts = (pl.ds(0, 128), pl.ds(128, HALF - 128))

    def c2o_copy(h, s, d):
        return rcopy(
            S2O.at[h, s, cuts[d]], R2O.at[h, s, cuts[d]], c2os.at[h, s, d], c2or.at[h, s, d], last_dev[s][d]
        )

    def c2m_copy(h, s, d, n):
        return rcopy(
            S2M.at[h, s, d, cuts[n]], R2M.at[h, s, d, cuts[n]], c2ms.at[h, s, d, n], c2mr.at[h, s, d, n], last_dev[s][d]
        )

    def c1(h):
        for s in range(2):
            c0_copy(h, s, 2).wait_recv()

            def fill(b, carry):
                S1O[h, s, b] = value(h, s, 2, b).astype(BF16)
                return carry

            lax.fori_loop(0, 4, fill, 0)
            for d in range(2):
                c1o_copy(h, s, d).start()
        for d in range(2):
            for s in range(2):
                o, n = (1, 3)[d], 1 - d
                c0_copy(h, s, o).wait_recv()

                def fill(b, carry):
                    S1M[h, s, d, b] = value(h, s, o, b).astype(BF16)
                    return carry

                lax.fori_loop(n * 2, n * 2 + 2, fill, 0)
                c1m_copy(h, s, d, n).start()

    def c2(h):
        for d in range(2):
            for s in range(2):
                o = (1, 3)[d]
                c1o_copy(h, s, d).wait_recv()

                def fill(b, carry):
                    S1M[h, s, d, b] = (value(h, s, o, b) + R1O[h, s, b].astype(F32)).astype(BF16)
                    return carry

                lax.fori_loop(d * 2, d * 2 + 2, fill, 0)
                c1m_copy(h, s, d, d).start()

    def c3(h):
        for s in range(2):
            c0_copy(h, s, 0).wait_recv()
            for d in range(2):
                for n in range(2):
                    c1m_copy(h, s, d, n).wait_recv()

            def fill(b, carry):
                A1[s, b] = value(h, s, 0, b) + R1M[h, s, 0, b].astype(F32) + R1M[h, s, 1, b].astype(F32)
                return carry

            lax.fori_loop(0, 4, fill, 0)
            S2O[h, s] = A1[s, rot(last_at[s], 2)].astype(BF16)
            for d in range(2):
                c2o_copy(h, s, d).start()
            for d in range(2):
                n = 1 - d
                S2M[h, s, d, cuts[n], :] = A1[s, rot(last_at[s], (1, 3)[d]), cuts[n], :].astype(BF16)
                c2m_copy(h, s, d, n).start()

    def c4(h):
        for s in range(2):
            for d in range(2):
                c2o_copy(h, s, d).wait_recv()
                relayed = A1[s, rot(last_at[s], (1, 3)[d]), cuts[d], :] + R2O[h, s, cuts[d], :].astype(F32)
                S2M[h, s, d, cuts[d], :] = relayed.astype(BF16)
                c2m_copy(h, s, d, d).start()

    def c5(h):
        for s in range(2):
            for d in range(2):
                for n in range(2):
                    c2m_copy(h, s, d, n).wait_recv()
            FIN[...] = A1[s, last_at[s]] + R2M[h, s, 0].astype(F32) + R2M[h, s, 1].astype(F32)
            for g in range(2):
                n = s * 2 + g
                mixed = FIN[g * ROWS : (g + 1) * ROWS, :] + NEWCTX[h, n * ROWS : (n + 1) * ROWS, :HD]
                sums = jnp.sum(jnp.where(eye, FIN[256 + g : 257 + g, :], 0.0), axis=1, keepdims=True)
                sums = sums + NEWCTX[h, n * ROWS : (n + 1) * ROWS, HD:]
                m = h * GROUP + n
                out[:, m * HD : (m + 1) * HD] = (mixed / sums).astype(BF16)

    def step(i, carry):
        def at_step(k):
            return pl.when(i == k)

        @pl.when(i < ITEMS - 2)
        def _():
            opposite(i + 2)

        @pl.when(i < ITEMS)
        def _():
            neighbours(i)

        @at_step(0)
        def _():
            q1_forward(0)

        @at_step(2)
        def _():
            q2_forward(0)
            q2_start(1)

        @pl.when(i >= 1)
        def _():
            own(i - 1)

        @at_step(0)
        def _():
            q2_start(0)

        @at_step(1)
        def _():
            q1_forward(1)

        @at_step(3)
        def _():
            q2_finish(0)
            w_wait(1)

        @at_step(4)
        def _():
            q2_forward(1)
            attend_new()

        @at_step(5)
        def _():
            q3_wait(0)
            attend_pages(0, 0, 6)

        @at_step(6)
        def _():
            attend_pages(0, 6, PAGES)
            c0(0)
            q2_finish(1)

        @at_step(7)
        def _():
            c1(0)

        @at_step(8)
        def _():
            q3_wait(1)
            attend_pages(1, 0, 4)
            c2(0)

        @pl.when(i >= 9)
        def _():
            attend_pages(1, 2 * (i - 7), 2 * (i - 6))

        for k, stage in ((9, c3), (10, c4), (11, c5)):

            @at_step(k)
            def _(stage=stage):
                stage(0)

        return carry

    lax.fori_loop(0, ITEMS + 1, step, 0)
    for o in range(4):
        for s in range(2):
            c0_copy(0, s, o).wait_send()
    for stage in (c0, c1, c2, c3, c4, c5):
        stage(1)

    for kv in range(2):
        for h in range(2):
            for e in (1, 2, 3):
                w1_copy(e, h, kv).wait_send()
            w_rings[h][kv].drain()
            for n in range(4):
                w3_copy(h, kv, c, n).wait_send()
    nh_ring.drain()
    for e in (1, 2, 3):
        rcopy(SSQ.at[z], SSQ.at[z], sqs.at[e], sqr.at[e], zdev[e]).wait_send()

    def drain(i, carry):
        for s in range(2):
            opp_copy(i, s).wait_send()
            mid_copy(i, s).wait_send()
        return carry

    lax.fori_loop(0, ITEMS, drain, 0)
    for o in range(4):
        for s in range(2):
            c0_copy(1, s, o).wait_send()
    for h in range(2):
        for s in range(2):
            q1[h][s].drain()
            q2[h][s].drain()
            for n in range(4):
                q3_copy(h, s, c, n).wait_send()
            for d in range(2):
                c1o_copy(h, s, d).wait_send()
                c2o_copy(h, s, d).wait_send()
                for n in range(2):
                    c1m_copy(h, s, d, n).wait_send()
                    c2m_copy(h, s, d, n).wait_send()


def local(store, new_hidden, wq, wk, wv, norm_gain, q_gain, k_gain, page_table, hist_len):
    tables = [jnp.asarray(t) for t in rope_tables()]
    vm = pl.BlockSpec(memory_space=pltpu.VMEM)
    hbm = pl.BlockSpec(memory_space=pl.ANY)
    dma = pltpu.SemaphoreType.DMA
    scratch = [
        pltpu.VMEM((PAGES, ROWS, FEAT), BF16),
        pltpu.VMEM((4, 2, 2, FEAT, HD), BF16),
        pltpu.VMEM((2, FEAT, 1024), BF16),
        pltpu.VMEM((2, FEAT, 256), BF16),
        pltpu.VMEM((2, FEAT, 256), BF16),
        pltpu.VMEM((ROWS, 1536), F32),
        pltpu.VMEM((4, ROWS, FEAT), BF16),
        pltpu.VMEM((4, 16, ROWS), F32),
        pltpu.VMEM((ROWS, ROWS), F32),
        pltpu.VMEM((ITEMS, 2, ROWS, 256), BF16),
        pltpu.VMEM((ITEMS, 2, ROWS, 256), BF16),
        pltpu.VMEM((ITEMS, 2, 2, ROWS, 256), BF16),
        pltpu.VMEM((ITEMS, 2, 2, ROWS, 256), BF16),
        pltpu.VMEM((2 * PAGES, ROWS, HD), BF16),
        pltpu.VMEM((2 * PAGES, ROWS, 2 * HD), BF16),
        pltpu.VMEM((2, QROWS, 2 * HD), F32),
        pltpu.VMEM((2, REQS, QROWS // 2, HD), BF16),
        pltpu.VMEM((2, REQS, QROWS // 2, HD), BF16),
        pltpu.VMEM((2, PAGES + 1, 2, HALF, HD), BF16),
        pltpu.VMEM((2, 4, 4, HALF, HD), BF16),
        pltpu.VMEM((2, 2, 4, 4, HALF, HD), BF16),
        pltpu.VMEM((2, 2, 4, HALF, HD), BF16),
        pltpu.VMEM((2, 2, 4, HALF, HD), BF16),
        pltpu.VMEM((2, 2, 2, 4, HALF, HD), BF16),
        pltpu.VMEM((2, 2, 2, 4, HALF, HD), BF16),
        pltpu.VMEM((2, 4, HALF, HD), F32),
        pltpu.VMEM((2, 2, HALF, HD), BF16),
        pltpu.VMEM((2, 2, HALF, HD), BF16),
        pltpu.VMEM((2, 2, 2, HALF, HD), BF16),
        pltpu.VMEM((2, 2, 2, HALF, HD), BF16),
        pltpu.VMEM((HALF, HD), F32),
        pltpu.VMEM((24, HD), jnp.int32),
        pltpu.SMEM((24, HD), jnp.int32),
        dma((8,)), dma((2, 3)),
        dma((2, 2, 4)), dma((2, 2, 4)), dma((2, 2, 4)), dma((2, 2, 4)), dma((2, 2, 4)), dma((2, 2, 4)),
        dma((4,)), dma((4,)), dma((4,)), dma((4,)),
        dma((ITEMS, 2)), dma((ITEMS, 2)), dma((ITEMS, 2)), dma((ITEMS, 2)),
        dma((2, 2, 4)), dma((2, 2, 4)), dma((2, 2, 4)), dma((2, 2, 4)), dma((2, 2, 4)), dma((2, 2, 4)),
        dma((2, 2, 4)), dma((2, 2, 4)),
        dma((2, 2, 2)), dma((2, 2, 2)), dma((2, 2, 2, 2)), dma((2, 2, 2, 2)),
        dma((2, 2, 2)), dma((2, 2, 2)), dma((2, 2, 2, 2)), dma((2, 2, 2, 2)),
    ]
    return pl.pallas_call(
        kernel,
        out_shape=jax.ShapeDtypeStruct((ROWS, 2 * GROUP * HD), BF16),
        in_specs=[vm, pl.BlockSpec(memory_space=pltpu.SMEM)] + [hbm] * 5 + [vm] * 7,
        out_specs=vm,
        scratch_shapes=scratch,
        compiler_params=pltpu.CompilerParams(
            collective_id=0, has_side_effects=True, vmem_limit_bytes=63 * 1024 * 1024
        ),
        cost_estimate=pl.CostEstimate(flops=12_000_000_000, bytes_accessed=25_000_000, transcendentals=2_000_000),
    )(
        page_table.T, hist_len, store, new_hidden, wq, wk, wv, norm_gain.reshape(WIDE // HD, HD),
        q_gain.reshape(1, HD), k_gain.reshape(1, HD), *tables,
    )


def solution(mesh):
    return jax.shard_map(
        local,
        mesh=mesh,
        in_specs=(
            P("pool", None, "tensor"),
            P("pool", "tensor"),
            P(None, "tensor"),
            P(None, "tensor"),
            P(None, "tensor"),
            P(),
            P(),
            P(),
            P(),
            P(),
        ),
        out_specs=P("pool", "tensor"),
        check_vma=False,
    )
```

time: 142 us -> 118 us (0.83)
  Pallas kernels: 130 us -> 115 us
  local copies, waits for them, and re-layouts: 6.57 us -> 1.67 us
  between operations: 2.66 us -> 0.01 us
    pallas_call x1, Pallas kernels: 130 us -> 115 us  [local(): pl.pallas_call(kernel, out_shape=jax.ShapeDtypeStruct((ROWS, 2 * GROUP *...]
    dynamic_slice x2 -> x0, local copies, waits for them, and re-layouts: 2.03 us -> none  [the longest x1 1.24 us: local(): lax.dynamic_index_in_dim(hist_len, p, 0, keepdims=False)]
where the time goes in v2:
time: 118 us; the launch traced here: 117 us
  Pallas kernels  115 us (97%)
  local copies, waits for them, and re-layouts  1.67 us (1%)
    pallas_call x1, Pallas kernels, local(): pl.pallas_call(kernel, out_shape=jax.ShapeDtypeStruct((ROWS, 2 * GROUP *...  115 us

profile of v2, /device:TPU:1, one launch (start us, length us, event | category | flops | bytes accessed | tf_op | source)
XLA Modules:
  0.0 117.0 jit_solution(4302603922050712699)
XLA Ops:
  0.0 115.4 %shard_map.136 = bf16[128,1024]{1,0:T(8,128)(2,1)} custom-call(s32[16,32]{1,0:T(8,128)} %bitcast.5, s32[32]{0:T(128)} %lengths.1, bf16[12,128,1280]{2,1,0:T(8,128)(2,1)} %store.1, bf16[128,1280]{1,0:T(8,128)(2,1)} %new_hidden.1, bf16[5120,1024]{1,0:T(8,128)(2,1)} %wq.1, bf16[5120,256]{1,0:T(8,128)(2,1)} %wk.1, bf16[5120,256]{1,0:T(8,128)(2,1)} %wv.1, ...), custom_call_target="tpu_custom_call" | custom-call | flops 12000000000 | bytes 25000000 | tf_op jit(solution)/shard_map/pallas_call | solution.py:771
  115.4 1.7 %copy.16 = bf16[128,1024]{1,0:T(8,128)(2,1)} copy(bf16[128,1024]{1,0:T(8,128)(2,1)} %shard_map.136) | data formatting | bytes 524288

commit v3 on v2

--- a/solution.py
+++ b/solution.py
@@ -71,6 +71,30 @@
         self.copy(self.half(self.right, 1), 3, self.down).wait_send()
 
 
+class Spread:
+    def __init__(self, piece, at, devs, send, recv):
+        self.piece, self.devs, self.send, self.recv = piece, devs, send, recv
+        self.places = [lax.rem(at + d, 4) for d in (0, 3, 1, 2)]
+
+    def copy(self, place, n):
+        ref = self.piece(place)
+        return pltpu.make_async_remote_copy(
+            src_ref=ref, dst_ref=ref, send_sem=self.send(n), recv_sem=self.recv(n),
+            device_id=self.devs[n], device_id_type=MESH,
+        )
+
+    def start(self):
+        for n in range(3):
+            self.copy(self.places[0], n).start()
+
+    def wait(self, n):
+        self.copy(self.places[n + 1], n).wait_recv()
+
+    def drain(self):
+        for n in range(3):
+            self.copy(self.places[0], n).wait_send()
+
+
 def nt(a, b):
     return lax.dot_general(a, b, (((1,), (1,)), ((), ())), preferred_element_type=F32)
 
@@ -80,12 +104,13 @@
 
 
 def kernel(
-    table, lengths, store, new_hidden, wq, wk, wv, norm_gain, q_gain, k_gain, cosr, sinr, cosp, sinp,
+    table_in, lengths, store, new_hidden, wq, wk, wv, norm_gain_in, q_gain_in, k_gain_in, cosr_in, sinr_in, cosp_in, sinp_in,
     out,
     X, W, WQB, WKB, WVB, ACC, NH, SSQ, INV, OPPS, OPPR, MIDS, MIDR, KB, VB, NEWCTX, QA, QB, CTX,
-    S0, R0, S1O, R1O, S1M, R1M, A1, S2O, R2O, S2M, R2M, FIN, TV, TS,
+    S0, R0, S1O, R1O, S1M, R1M, A1, S2M, R2M, FIN, TV, TS,
+    table, norm_gain, q_gain, k_gain, cosr, sinr, cosp, sinp,
     lsem, wbsem, w1s, w1r, w2s, w2r, w3s, w3r, nhs, nhr, sqs, sqr, os_, or_, ms, mr,
-    q1s, q1r, q2s, q2r, q3s, q3r, c0s, c0r, c1os, c1or, c1ms, c1mr, c2os, c2or, c2ms, c2mr,
+    q1s, q1r, q2s, q2r, q3s, q3r, c0s, c0r, c1os, c1or, c1ms, c1mr, c2s, c2r,
 ):
     QS = (QA, QB)
     p = lax.axis_index("pool")
@@ -105,6 +130,8 @@
     xup, xdn = (at(y, rot(x, 1), c), z), (at(y, rot(x, 3), c), z)
     yup, ydn = (at(rot(y, 1), x, c), z), (at(rot(y, 3), x, c), z)
     sib = (at(y, x, oc), z)
+    xall = (xup, xdn, (at(y, rot(x, 2), c), z))
+    yall = (yup, ydn, (at(rot(y, 2), x, c), z))
 
     def rcopy(src, dst, ss, rs, dev):
         return pltpu.make_async_remote_copy(
@@ -117,11 +144,68 @@
     for cp in ld_x:
         cp.start()
 
+    small = [
+        (table_in, table), (norm_gain_in, norm_gain), (q_gain_in, q_gain), (k_gain_in, k_gain),
+        (cosr_in, cosr), (sinr_in, sinr), (cosp_in, cosp), (sinp_in, sinp),
+    ]
+    ld_small = [pltpu.make_async_copy(src, dst, lsem.at[8 + n]) for n, (src, dst) in enumerate(small)]
+    for cp in ld_small:
+        cp.start()
+
     barrier = pltpu.get_barrier_semaphore()
-    peers = [zdev[1], zdev[2], zdev[3], xup, xdn, yup, ydn, sib]
+    peers = [*zdev[1:], *xall, *yall, sib]
     for dev in peers:
         pl.semaphore_signal(barrier, inc=1, device_id=dev, device_id_type=MESH)
 
+    def block_loads(d):
+        rows = pl.ds(pl.multiple_of(rot(z, d) * FEAT, FEAT), FEAT)
+        b = (0, 1, 1, 0)[d]
+        return [
+            pltpu.make_async_copy(wq.at[rows, :], WQB.at[b], wbsem.at[b, 0]),
+            pltpu.make_async_copy(wk.at[rows, :], WKB.at[b], wbsem.at[b, 1]),
+            pltpu.make_async_copy(wv.at[rows, :], WVB.at[b], wbsem.at[b, 2]),
+        ]
+
+    own_rows = pl.ds(pl.multiple_of(z * FEAT, FEAT), FEAT)
+    ld_w = []
+    for h in range(2):
+        for kv, ref in enumerate((wk, wv)):
+            ld_w.append(
+                pltpu.make_async_copy(
+                    ref.at[own_rows, h * HD : (h + 1) * HD], W.at[0, h, kv], lsem.at[4 + 2 * h + kv]
+                )
+            )
+
+    pl.semaphore_wait(barrier, len(peers))
+    ring_at = (x, y)
+
+    def seg_rows(cc, k):
+        return pl.ds(pl.multiple_of(cc * (4 * SEG) + k * SEG, SEG), SEG)
+
+    def w1_copy(e, h, kv):
+        ref = (wk, wv)[kv]
+        seg = pl.multiple_of(c * (4 * SEG) + ring_at[kv] * SEG, SEG)
+        src = ref.at[pl.ds(pl.multiple_of(rot(z, e) * FEAT + seg, SEG), SEG), h * HD : (h + 1) * HD]
+        return rcopy(src, W.at[4 - e, h, kv, pl.ds(seg, SEG), :], w1s.at[kv, h, e], w1r.at[kv, h, 4 - e], zdev[e])
+
+    nh_ring = Ring(
+        lambda k: NH.at[k], lambda k, s: NH.at[k, pl.ds(64 * s, 64), :], z, zdev[1], zdev[3],
+        lambda k: nhs.at[k], lambda k: nhr.at[k],
+    )
+    def w1_start(h):
+        for kv in range(2):
+            for e in (2, 1, 3):
+                w1_copy(e, h, kv).start()
+
+    w1_start(0)
+
+    def w1_wait(slot, h, kv):
+        seg = pl.multiple_of(c * (4 * SEG) + ring_at[kv] * SEG, SEG)
+        dst = W.at[slot, h, kv, pl.ds(seg, SEG), :]
+        rcopy(dst, dst, w1s.at[kv, h, slot], w1r.at[kv, h, slot], zdev[slot]).wait_recv()
+
+    for cp in ld_small:
+        cp.wait()
     page = table[...] - p * PAGES
     hit = jnp.logical_and(page >= 0, page < PAGES)
     rank = lax.broadcasted_iota(jnp.int32, (16, REQS), 0)
@@ -140,7 +224,10 @@
     lane = lax.broadcasted_iota(jnp.int32, (ROWS, ROWS), 1)
     row = lax.broadcasted_iota(jnp.int32, (ROWS, ROWS), 0)
     eye = lane == row
-    gain = jnp.concatenate([norm_gain[pl.ds(z * (FEAT // HD) + k, 1), :] for k in range(FEAT // HD)], axis=1)
+
+    def gain_of(zz):
+        return jnp.concatenate([norm_gain[pl.ds(zz * (FEAT // HD) + k, 1), :] for k in range(FEAT // HD)], axis=1)
+
 
     def squares_of(v):
         v = v.astype(F32)
@@ -154,51 +241,11 @@
             6 * n, 6 * n + 6, lambda j, acc: jnp.where(lane == j, squares_of(X[j]), acc), squares
         )
     SSQ[z] = jnp.transpose(squares)[:16, :]
-    to_scalar.wait()
-
-    def block_loads(d):
-        rows = pl.ds(pl.multiple_of(rot(z, d) * FEAT, FEAT), FEAT)
-        b = (0, 1, 1, 0)[d]
-        return [
-            pltpu.make_async_copy(wq.at[rows, :], WQB.at[b], wbsem.at[b, 0]),
-            pltpu.make_async_copy(wk.at[rows, :], WKB.at[b], wbsem.at[b, 1]),
-            pltpu.make_async_copy(wv.at[rows, :], WVB.at[b], wbsem.at[b, 2]),
-        ]
-
-    own_rows = pl.ds(pl.multiple_of(z * FEAT, FEAT), FEAT)
-    ld_w = []
-    for h in range(2):
-        for kv, ref in enumerate((wk, wv)):
-            ld_w.append(
-                pltpu.make_async_copy(
-                    ref.at[own_rows, h * HD : (h + 1) * HD], W.at[0, h, kv], lsem.at[4 + 2 * h + kv]
-                )
-            )
-
-    pl.semaphore_wait(barrier, len(peers))
     for e in (1, 2, 3):
         rcopy(SSQ.at[z], SSQ.at[z], sqs.at[e], sqr.at[e], zdev[e]).start()
-
-    ring_at = (x, y)
-
-    def seg_rows(cc, k):
-        return pl.ds(pl.multiple_of(cc * (4 * SEG) + k * SEG, SEG), SEG)
-
-    def w1_copy(e, h, kv):
-        ref = (wk, wv)[kv]
-        seg = pl.multiple_of(c * (4 * SEG) + ring_at[kv] * SEG, SEG)
-        src = ref.at[pl.ds(pl.multiple_of(rot(z, e) * FEAT + seg, SEG), SEG), h * HD : (h + 1) * HD]
-        return rcopy(src, W.at[4 - e, h, kv, pl.ds(seg, SEG), :], w1s.at[kv, h, e], w1r.at[kv, h, 4 - e], zdev[e])
-
-    for h in range(2):
-        for kv in range(2):
-            for e in (2, 1, 3):
-                w1_copy(e, h, kv).start()
-
-    def w1_wait(slot, h, kv):
-        seg = pl.multiple_of(c * (4 * SEG) + ring_at[kv] * SEG, SEG)
-        dst = W.at[slot, h, kv, pl.ds(seg, SEG), :]
-        rcopy(dst, dst, w1s.at[kv, h, slot], w1r.at[kv, h, slot], zdev[slot]).wait_recv()
+    nh_ring.start()
+    w1_start(1)
+    to_scalar.wait()
 
     for d in (0, 1):
         for cp in block_loads(d):
@@ -206,72 +253,40 @@
     for cp in ld_w:
         cp.start()
 
-    for e in (1, 2, 3):
-        far = SSQ.at[rot(z, 4 - e)]
-        rcopy(far, far, sqs.at[e], sqr.at[e], zdev[e]).wait_recv()
-    total = SSQ[0] + SSQ[1] + SSQ[2] + SSQ[3]
-    inverse = lax.rsqrt(total * (1.0 / WIDE) + EPS)
-    INV[...] = jnp.transpose(jnp.concatenate([inverse, jnp.zeros((ROWS - 16, ROWS), F32)], axis=0))
-
-    def normed(v, j):
+    def normed(v, j, gain):
         inv = jnp.sum(jnp.where(lane == j, INV[...], 0.0), axis=1, keepdims=True)
         return (v.astype(F32) * inv * gain).astype(BF16)
 
-    NH[z] = normed(NH[z], PAGES)
-    nh_ring = Ring(
-        lambda k: NH.at[k], lambda k, s: NH.at[k, pl.ds(64 * s, 64), :], z, zdev[1], zdev[3],
-        lambda k: nhs.at[k], lambda k: nhr.at[k],
-    )
-    nh_ring.start()
-
     def prepare(j, carry):
-        X[j] = normed(X[j], j)
+        X[j] = normed(X[j], j, gain)
         return carry
-
-    lax.fori_loop(0, PAGES, prepare, 0)
 
     def w_piece(h, kv, cc):
         return lambda k: W.at[pl.ds(1, 3), h, kv, seg_rows(cc, k), :]
 
-    def w_half(h, kv):
-        def half(k, s):
-            first = pl.multiple_of(c * (4 * SEG) + k * SEG + s * (SEG // 2), SEG // 2)
-            return W.at[pl.ds(1, 3), h, kv, pl.ds(first, SEG // 2), :]
-
-        return half
-
-    def w_ring_of(h, kv):
-        up, down = ((xup, xdn), (yup, ydn))[kv]
-        return Ring(
-            w_piece(h, kv, c), w_half(h, kv), ring_at[kv], up, down,
-            lambda k: w2s.at[h, kv, k], lambda k: w2r.at[h, kv, k],
-        )
-
-    w_rings = [[w_ring_of(h, kv) for kv in range(2)] for h in range(2)]
+    def w_spread_of(h, kv):
+        return Spread(
+            w_piece(h, kv, c), ring_at[kv], (xall, yall)[kv], lambda n: w2s.at[h, kv, n], lambda n: w2r.at[h, kv, n]
+        )
+
+    w_spread = [[w_spread_of(h, kv) for kv in range(2)] for h in range(2)]
 
     def w3_copy(h, kv, cc, n):
-        ring = w_rings[h][kv]
-        ref = w_piece(h, kv, cc)((ring.at, ring.left, ring.right, ring.opp)[n])
+        ref = w_piece(h, kv, cc)(w_spread[h][kv].places[n])
         return rcopy(ref, ref, w3s.at[h, kv, n], w3r.at[h, kv, n], sib)
 
     def w_start(h):
         for kv in range(2):
             for slot in (1, 2, 3):
                 w1_wait(slot, h, kv)
-            w_rings[h][kv].start()
+            w_spread[h][kv].start()
             w3_copy(h, kv, c, 0).start()
 
-    def w_forward(h):
-        for kv in range(2):
-            w_rings[h][kv].forward_left()
-            w3_copy(h, kv, c, 1).start()
-            w_rings[h][kv].forward_right()
-            w3_copy(h, kv, c, 2).start()
-
-    def w_finish(h):
-        for kv in range(2):
-            w_rings[h][kv].finish()
-            w3_copy(h, kv, c, 3).start()
+    def w_share(h):
+        for n in range(3):
+            for kv in range(2):
+                w_spread[h][kv].wait(n)
+                w3_copy(h, kv, c, n + 1).start()
 
     def w_wait(h):
         for kv in range(2):
@@ -293,7 +308,7 @@
         for cp in block_loads(d):
             cp.wait()
         b = (0, 1, 1, 0)[d]
-        a = NH[rot(z, d)]
+        a = normed(NH[rot(z, d)], PAGES, gain_of(rot(z, d)))
         parts = ((0, WQB), (1024, WKB), (1280, WVB))
         for first, ref in parts:
             width = ref.shape[2]
@@ -307,15 +322,19 @@
                 cp.start()
 
     w_start(0)
+    for e in (1, 2, 3):
+        far = SSQ.at[rot(z, 4 - e)]
+        rcopy(far, far, sqs.at[e], sqr.at[e], zdev[e]).wait_recv()
+    total = SSQ[0] + SSQ[1] + SSQ[2] + SSQ[3]
+    inverse = lax.rsqrt(total * (1.0 / WIDE) + EPS)
+    INV[...] = jnp.transpose(jnp.concatenate([inverse, jnp.zeros((ROWS - 16, ROWS), F32)], axis=0))
+
+    gain = gain_of(z)
+    lax.fori_loop(0, PAGES, prepare, 0)
     project_new(0)
-    w_start(1)
-    w_forward(0)
     nh_ring.forward_left()
     nh_ring.forward_right()
-    project_new(1)
-    project_new(3)
-    w_finish(0)
-    w_forward(1)
+    w_share(0)
     w_wait(0)
 
     def product(i, slot):
@@ -388,82 +407,65 @@
 
         lax.fori_loop(first, last, one, 0)
 
-    opposite(0)
-    opposite(1)
-    w_finish(1)
-    nh_ring.finish()
-    project_new(2)
-    length = lengths[p]
-    page_cos, page_sin = cosp[pl.ds(length // ROWS, 1), :], sinp[pl.ds(length // ROWS, 1), :]
-    rest_cos, rest_sin = cosr[pl.ds(lax.rem(length, ROWS), 1), :], sinr[pl.ds(lax.rem(length, ROWS), 1), :]
-    cos_new, sin_new = angle_at(
-        page_cos * rest_cos - page_sin * rest_sin, page_sin * rest_cos + page_cos * rest_sin
-    )
-
     q_at = (c * 16 + y * 4 + x, c * 16 + x * 4 + y)
 
-    def q1_ring_of(h, s):
+    def q1_of(h, s):
         base = c * 16 + (y * 4, x * 4)[s]
-        up, down = ((xup, xdn), (yup, ydn))[s]
-        return Ring(
-            lambda k: QS[h].at[s, base + k],
-            lambda k, t: QS[h].at[s, base + k, pl.ds(t * 128, 128), :],
-            (x, y)[s], up, down, lambda k: q1s.at[h, s, k], lambda k: q1r.at[h, s, k],
-        )
-
-    def q2_ring_of(h, s):
-        up, down = ((yup, ydn), (xup, xdn))[s]
-        return Ring(
-            lambda k: QS[h].at[s, pl.ds(c * 16 + k * 4, 4)],
-            lambda k, t: QS[h].at[s, pl.ds(c * 16 + k * 4 + t * 2, 2)],
-            (y, x)[s], up, down, lambda k: q2s.at[h, s, k], lambda k: q2r.at[h, s, k],
-        )
-
-    q1 = [[q1_ring_of(h, s) for s in range(2)] for h in range(2)]
-    q2 = [[q2_ring_of(h, s) for s in range(2)] for h in range(2)]
+        return Spread(
+            lambda k: QS[h].at[s, base + k], (x, y)[s], (xall, yall)[s], lambda n: q1s.at[h, s, n], lambda n: q1r.at[h, s, n]
+        )
+
+    def q2_of(h, s):
+        return Spread(
+            lambda k: QS[h].at[s, pl.ds(c * 16 + k * 4, 4)], (y, x)[s], (yall, xall)[s],
+            lambda n: q2s.at[h, s, n], lambda n: q2r.at[h, s, n],
+        )
+
+    q1 = [[q1_of(h, s) for s in range(2)] for h in range(2)]
+    q2 = [[q2_of(h, s) for s in range(2)] for h in range(2)]
 
     def q3_copy(h, s, cc, n):
-        k = (q2[h][s].at, q2[h][s].left, q2[h][s].right, q2[h][s].opp)[n]
-        ref = QS[h].at[s, pl.ds(cc * 16 + k * 4, 4)]
+        ref = QS[h].at[s, pl.ds(cc * 16 + q2[h][s].places[n] * 4, 4)]
         return rcopy(ref, ref, q3s.at[h, s, n], q3r.at[h, s, n], sib)
 
-    for h in range(2):
-        for s in range(2):
-            for g in range(2):
-                n = h * GROUP + s * 2 + g
-                raw = ACC[:, n * HD : (n + 1) * HD]
-                QS[h][s, q_at[s], g * ROWS : (g + 1) * ROWS, :] = normed_rope(raw, q_gain[...], cos_new, sin_new)
-            q1[h][s].start()
-
-    def q1_forward(h):
-        for s in range(2):
-            q1[h][s].forward_left()
-            q1[h][s].forward_right()
-
-    def q2_start(h):
-        for s in range(2):
-            q1[h][s].finish()
+    def angles_new():
+        length = lengths[p]
+        page_cos, page_sin = cosp[pl.ds(length // ROWS, 1), :], sinp[pl.ds(length // ROWS, 1), :]
+        rest_cos, rest_sin = cosr[pl.ds(lax.rem(length, ROWS), 1), :], sinr[pl.ds(lax.rem(length, ROWS), 1), :]
+        return angle_at(page_cos * rest_cos - page_sin * rest_sin, page_sin * rest_cos + page_cos * rest_sin)
+
+    def q_begin():
+        nh_ring.finish()
+        project_new(2)
+        cos_new, sin_new = angles_new()
+        for h in range(2):
+            for s in range(2):
+                for g in range(2):
+                    n = h * GROUP + s * 2 + g
+                    raw = ACC[:, n * HD : (n + 1) * HD]
+                    QS[h][s, q_at[s], g * ROWS : (g + 1) * ROWS, :] = normed_rope(raw, q_gain[...], cos_new, sin_new)
+                q1[h][s].start()
+
+    def q_along(h):
+        for s in range(2):
+            for n in range(3):
+                q1[h][s].wait(n)
             q2[h][s].start()
             q3_copy(h, s, c, 0).start()
 
-    def q2_forward(h):
-        for s in range(2):
-            q2[h][s].forward_left()
-            q3_copy(h, s, c, 1).start()
-            q2[h][s].forward_right()
-            q3_copy(h, s, c, 2).start()
-
-    def q2_finish(h):
-        for s in range(2):
-            q2[h][s].finish()
-            q3_copy(h, s, c, 3).start()
-
-    def q3_wait(h):
+    def q_share(h):
+        for n in range(3):
+            for s in range(2):
+                q2[h][s].wait(n)
+                q3_copy(h, s, c, n + 1).start()
+
+    def q_wait(h):
         for s in range(2):
             for n in range(4):
                 q3_copy(h, s, oc, n).wait_recv()
 
     def attend_new():
+        cos_new, sin_new = angles_new()
         causal = lax.broadcasted_iota(jnp.int32, (QROWS, ROWS), 1) <= (
             lax.broadcasted_iota(jnp.int32, (QROWS, ROWS), 0) & (ROWS - 1)
         )
@@ -477,7 +479,7 @@
             NEWCTX[h] = nn(weights, jnp.concatenate([val, ones], axis=1))
 
     first_dev = ((xup, xdn), (yup, ydn))
-    last_dev = ((yup, ydn), (xup, xdn))
+    last_dev = (yall, xall)
     first_at, last_at = (x, y), (y, x)
 
     def mine(h, s, o, b, core):
@@ -512,17 +514,8 @@
             S1M.at[h, s, d, part], R1M.at[h, s, d, part], c1ms.at[h, s, d, n], c1mr.at[h, s, d, n], first_dev[s][d]
         )
 
-    cuts = (pl.ds(0, 128), pl.ds(128, HALF - 128))
-
-    def c2o_copy(h, s, d):
-        return rcopy(
-            S2O.at[h, s, cuts[d]], R2O.at[h, s, cuts[d]], c2os.at[h, s, d], c2or.at[h, s, d], last_dev[s][d]
-        )
-
-    def c2m_copy(h, s, d, n):
-        return rcopy(
-            S2M.at[h, s, d, cuts[n]], R2M.at[h, s, d, cuts[n]], c2ms.at[h, s, d, n], c2mr.at[h, s, d, n], last_dev[s][d]
-        )
+    def c2_copy(h, s, n):
+        return rcopy(S2M.at[h, s, n], R2M.at[h, s, n], c2s.at[h, s, n], c2r.at[h, s, n], last_dev[s][n])
 
     def c1(h):
         for s in range(2):
@@ -572,28 +565,16 @@
                 return carry
 
             lax.fori_loop(0, 4, fill, 0)
-            S2O[h, s] = A1[s, rot(last_at[s], 2)].astype(BF16)
-            for d in range(2):
-                c2o_copy(h, s, d).start()
-            for d in range(2):
-                n = 1 - d
-                S2M[h, s, d, cuts[n], :] = A1[s, rot(last_at[s], (1, 3)[d]), cuts[n], :].astype(BF16)
-                c2m_copy(h, s, d, n).start()
+            for n, o in ((2, 2), (0, 1), (1, 3)):
+                S2M[h, s, n] = A1[s, rot(last_at[s], o)].astype(BF16)
+                c2_copy(h, s, n).start()
 
     def c4(h):
         for s in range(2):
-            for d in range(2):
-                c2o_copy(h, s, d).wait_recv()
-                relayed = A1[s, rot(last_at[s], (1, 3)[d]), cuts[d], :] + R2O[h, s, cuts[d], :].astype(F32)
-                S2M[h, s, d, cuts[d], :] = relayed.astype(BF16)
-                c2m_copy(h, s, d, d).start()
-
-    def c5(h):
-        for s in range(2):
-            for d in range(2):
-                for n in range(2):
-                    c2m_copy(h, s, d, n).wait_recv()
-            FIN[...] = A1[s, last_at[s]] + R2M[h, s, 0].astype(F32) + R2M[h, s, 1].astype(F32)
+            for n in range(3):
+                c2_copy(h, s, n).wait_recv()
+            parts = R2M[h, s, 0].astype(F32) + R2M[h, s, 1].astype(F32) + R2M[h, s, 2].astype(F32)
+            FIN[...] = A1[s, last_at[s]] + parts
             for g in range(2):
                 n = s * 2 + g
                 mixed = FIN[g * ROWS : (g + 1) * ROWS, :] + NEWCTX[h, n * ROWS : (n + 1) * ROWS, :HD]
@@ -602,9 +583,18 @@
                 m = h * GROUP + n
                 out[:, m * HD : (m + 1) * HD] = (mixed / sums).astype(BF16)
 
+    opposite(0)
+    opposite(1)
+    w_start(1)
+    project_new(1)
+    project_new(3)
+
     def step(i, carry):
-        def at_step(k):
-            return pl.when(i == k)
+        def at_step(k, *actions):
+            @pl.when(i == k)
+            def _():
+                for action in actions:
+                    action()
 
         @pl.when(i < ITEMS - 2)
         def _():
@@ -614,82 +604,49 @@
         def _():
             neighbours(i)
 
-        @at_step(0)
+        @pl.when(i >= 2)
         def _():
-            q1_forward(0)
-
-        @at_step(2)
-        def _():
-            q2_forward(0)
-            q2_start(1)
-
-        @pl.when(i >= 1)
-        def _():
-            own(i - 1)
-
-        @at_step(0)
-        def _():
-            q2_start(0)
-
-        @at_step(1)
-        def _():
-            q1_forward(1)
-
-        @at_step(3)
-        def _():
-            q2_finish(0)
-            w_wait(1)
-
-        @at_step(4)
-        def _():
-            q2_forward(1)
-            attend_new()
-
-        @at_step(5)
-        def _():
-            q3_wait(0)
-            attend_pages(0, 0, 6)
-
-        @at_step(6)
-        def _():
-            attend_pages(0, 6, PAGES)
-            c0(0)
-            q2_finish(1)
-
-        @at_step(7)
-        def _():
-            c1(0)
-
-        @at_step(8)
-        def _():
-            q3_wait(1)
-            attend_pages(1, 0, 4)
-            c2(0)
-
-        @pl.when(i >= 9)
-        def _():
-            attend_pages(1, 2 * (i - 7), 2 * (i - 6))
-
-        for k, stage in ((9, c3), (10, c4), (11, c5)):
-
-            @at_step(k)
-            def _(stage=stage):
-                stage(0)
-
+            own(i - 2)
+
+        def pages(h, first, last):
+            return lambda: attend_pages(h, first, last)
+
+        def of(stage, h):
+            return lambda: stage(h)
+
+        at_step(0, q_begin)
+        at_step(1, of(w_share, 1))
+        at_step(2, of(q_along, 0))
+        at_step(3, of(w_wait, 1), attend_new)
+        at_step(4, of(q_along, 1))
+        at_step(5, of(q_share, 0))
+        at_step(6, of(q_wait, 0), pages(0, 0, 4))
+        at_step(7, pages(0, 4, 8))
+        at_step(8, pages(0, 8, 12), of(c0, 0), of(q_share, 1))
+        at_step(9, of(c1, 0), of(q_wait, 1), pages(1, 0, 2))
+        at_step(10, pages(1, 2, 5))
+        at_step(11, of(c2, 0), pages(1, 5, 8))
+        at_step(12, pages(1, 8, 10))
+        at_step(13, pages(1, 10, 12))
         return carry
 
-    lax.fori_loop(0, ITEMS + 1, step, 0)
+    lax.fori_loop(0, ITEMS + 2, step, 0)
     for o in range(4):
         for s in range(2):
             c0_copy(0, s, o).wait_send()
-    for stage in (c0, c1, c2, c3, c4, c5):
-        stage(1)
+    c0(1)
+    c3(0)
+    c1(1)
+    c2(1)
+    c4(0)
+    c3(1)
+    c4(1)
 
     for kv in range(2):
         for h in range(2):
             for e in (1, 2, 3):
                 w1_copy(e, h, kv).wait_send()
-            w_rings[h][kv].drain()
+            w_spread[h][kv].drain()
             for n in range(4):
                 w3_copy(h, kv, c, n).wait_send()
     nh_ring.drain()
@@ -714,10 +671,10 @@
                 q3_copy(h, s, c, n).wait_send()
             for d in range(2):
                 c1o_copy(h, s, d).wait_send()
-                c2o_copy(h, s, d).wait_send()
                 for n in range(2):
                     c1m_copy(h, s, d, n).wait_send()
-                    c2m_copy(h, s, d, n).wait_send()
+            for n in range(3):
+                c2_copy(h, s, n).wait_send()
 
 
 def local(store, new_hidden, wq, wk, wv, norm_gain, q_gain, k_gain, page_table, hist_len):
@@ -752,26 +709,32 @@
         pltpu.VMEM((2, 2, 2, 4, HALF, HD), BF16),
         pltpu.VMEM((2, 2, 2, 4, HALF, HD), BF16),
         pltpu.VMEM((2, 4, HALF, HD), F32),
-        pltpu.VMEM((2, 2, HALF, HD), BF16),
-        pltpu.VMEM((2, 2, HALF, HD), BF16),
-        pltpu.VMEM((2, 2, 2, HALF, HD), BF16),
-        pltpu.VMEM((2, 2, 2, HALF, HD), BF16),
+        pltpu.VMEM((2, 2, 3, HALF, HD), BF16),
+        pltpu.VMEM((2, 2, 3, HALF, HD), BF16),
         pltpu.VMEM((HALF, HD), F32),
         pltpu.VMEM((24, HD), jnp.int32),
         pltpu.SMEM((24, HD), jnp.int32),
-        dma((8,)), dma((2, 3)),
+        pltpu.VMEM((16, REQS), jnp.int32),
+        pltpu.VMEM((WIDE // HD, HD), F32),
+        pltpu.VMEM((1, HD), F32),
+        pltpu.VMEM((1, HD), F32),
+        pltpu.VMEM((ROWS, HD), F32),
+        pltpu.VMEM((ROWS, HD), F32),
+        pltpu.VMEM((24, HD), F32),
+        pltpu.VMEM((24, HD), F32),
+        dma((16,)), dma((2, 3)),
         dma((2, 2, 4)), dma((2, 2, 4)), dma((2, 2, 4)), dma((2, 2, 4)), dma((2, 2, 4)), dma((2, 2, 4)),
         dma((4,)), dma((4,)), dma((4,)), dma((4,)),
         dma((ITEMS, 2)), dma((ITEMS, 2)), dma((ITEMS, 2)), dma((ITEMS, 2)),
         dma((2, 2, 4)), dma((2, 2, 4)), dma((2, 2, 4)), dma((2, 2, 4)), dma((2, 2, 4)), dma((2, 2, 4)),
         dma((2, 2, 4)), dma((2, 2, 4)),
         dma((2, 2, 2)), dma((2, 2, 2)), dma((2, 2, 2, 2)), dma((2, 2, 2, 2)),
-        dma((2, 2, 2)), dma((2, 2, 2)), dma((2, 2, 2, 2)), dma((2, 2, 2, 2)),
+        dma((2, 2, 3)), dma((2, 2, 3)),
     ]
     return pl.pallas_call(
         kernel,
         out_shape=jax.ShapeDtypeStruct((ROWS, 2 * GROUP * HD), BF16),
-        in_specs=[vm, pl.BlockSpec(memory_space=pltpu.SMEM)] + [hbm] * 5 + [vm] * 7,
+        in_specs=[hbm, pl.BlockSpec(memory_space=pltpu.SMEM)] + [hbm] * 12,
         out_specs=vm,
         scratch_shapes=scratch,
         compiler_params=pltpu.CompilerParams(

time: 118 us -> 109 us (0.924)
  Pallas kernels: 115 us -> 107 us
    pallas_call x1, Pallas kernels: 115 us -> 107 us  [local(): pl.pallas_call(kernel, out_shape=jax.ShapeDtypeStruct((ROWS, 2 * GROUP *...]
where the time goes in v3:
time: 109 us
  Pallas kernels  107 us (98%)
  local copies, waits for them, and re-layouts  1.67 us (2%)
    pallas_call x1, Pallas kernels, local(): pl.pallas_call(kernel, out_shape=jax.ShapeDtypeStruct((ROWS, 2 * GROUP *...  107 us

profile of v3, /device:TPU:1, one launch (start us, length us, event | category | flops | bytes accessed | tf_op | source)
XLA Modules:
  0.0 109.1 jit_solution(4978203279331984871)
XLA Ops:
  0.0 107.4 %shard_map.136 = bf16[128,1024]{1,0:T(8,128)(2,1)} custom-call(s32[16,32]{1,0:T(8,128)} %bitcast.5, s32[32]{0:T(128)} %lengths.1, bf16[12,128,1280]{2,1,0:T(8,128)(2,1)} %store.1, bf16[128,1280]{1,0:T(8,128)(2,1)} %new_hidden.1, bf16[5120,1024]{1,0:T(8,128)(2,1)} %wq.1, bf16[5120,256]{1,0:T(8,128)(2,1)} %wk.1, bf16[5120,256]{1,0:T(8,128)(2,1)} %wv.1, ...), custom_call_target="tpu_custom_call" | custom-call | flops 12000000000 | bytes 25000000 | tf_op jit(solution)/shard_map/pallas_call | solution.py:734
  107.4 1.7 %copy.16 = bf16[128,1024]{1,0:T(8,128)(2,1)} copy(bf16[128,1024]{1,0:T(8,128)(2,1)} %shard_map.136) | data formatting | bytes 524288

commit v4 on v3

--- a/solution.py
+++ b/solution.py
@@ -107,7 +107,7 @@
     table_in, lengths, store, new_hidden, wq, wk, wv, norm_gain_in, q_gain_in, k_gain_in, cosr_in, sinr_in, cosp_in, sinp_in,
     out,
     X, W, WQB, WKB, WVB, ACC, NH, SSQ, INV, OPPS, OPPR, MIDS, MIDR, KB, VB, NEWCTX, QA, QB, CTX,
-    S0, R0, S1O, R1O, S1M, R1M, A1, S2M, R2M, FIN, TV, TS,
+    S0, R0, S1O, R1O, S1M, R1M, A1, R2M, FIN, TV, TS,
     table, norm_gain, q_gain, k_gain, cosr, sinr, cosp, sinp,
     lsem, wbsem, w1s, w1r, w2s, w2r, w3s, w3r, nhs, nhr, sqs, sqr, os_, or_, ms, mr,
     q1s, q1r, q2s, q2r, q3s, q3r, c0s, c0r, c1os, c1or, c1ms, c1mr, c2s, c2r,
@@ -488,7 +488,7 @@
         return CTX[h, TS[0, chip * 2 + core], s]
 
     def value(h, s, o, b):
-        return mine(h, s, o, b, c).astype(F32) + R0[h, s, o, b].astype(F32)
+        return mine(h, s, o, b, c) + R0[h, s, o, b]
 
     def c0_copy(h, s, o):
         return rcopy(S0.at[s, o], R0.at[h, s, o], c0s.at[h, s, o], c0r.at[h, s, o], sib)
@@ -515,14 +515,15 @@
         )
 
     def c2_copy(h, s, n):
-        return rcopy(S2M.at[h, s, n], R2M.at[h, s, n], c2s.at[h, s, n], c2r.at[h, s, n], last_dev[s][n])
+        src = A1.at[h, s, (1, 3, 2)[n]]
+        return rcopy(src, R2M.at[h, s, n], c2s.at[h, s, n], c2r.at[h, s, n], last_dev[s][n])
 
     def c1(h):
         for s in range(2):
             c0_copy(h, s, 2).wait_recv()
 
             def fill(b, carry):
-                S1O[h, s, b] = value(h, s, 2, b).astype(BF16)
+                S1O[h, s, b] = value(h, s, 2, b)
                 return carry
 
             lax.fori_loop(0, 4, fill, 0)
@@ -534,7 +535,7 @@
                 c0_copy(h, s, o).wait_recv()
 
                 def fill(b, carry):
-                    S1M[h, s, d, b] = value(h, s, o, b).astype(BF16)
+                    S1M[h, s, d, b] = value(h, s, o, b)
                     return carry
 
                 lax.fori_loop(n * 2, n * 2 + 2, fill, 0)
@@ -547,7 +548,7 @@
                 c1o_copy(h, s, d).wait_recv()
 
                 def fill(b, carry):
-                    S1M[h, s, d, b] = (value(h, s, o, b) + R1O[h, s, b].astype(F32)).astype(BF16)
+                    S1M[h, s, d, b] = value(h, s, o, b) + R1O[h, s, b]
                     return carry
 
                 lax.fori_loop(d * 2, d * 2 + 2, fill, 0)
@@ -560,21 +561,18 @@
                 for n in range(2):
                     c1m_copy(h, s, d, n).wait_recv()
 
-            def fill(b, carry):
-                A1[s, b] = value(h, s, 0, b) + R1M[h, s, 0, b].astype(F32) + R1M[h, s, 1, b].astype(F32)
-                return carry
-
-            lax.fori_loop(0, 4, fill, 0)
-            for n, o in ((2, 2), (0, 1), (1, 3)):
-                S2M[h, s, n] = A1[s, rot(last_at[s], o)].astype(BF16)
-                c2_copy(h, s, n).start()
+            for n, o in ((2, 2), (0, 1), (1, 3), (None, 0)):
+                b = rot(last_at[s], o)
+                A1[h, s, o] = value(h, s, 0, b) + R1M[h, s, 0, b] + R1M[h, s, 1, b]
+                if n is not None:
+                    c2_copy(h, s, n).start()
 
     def c4(h):
         for s in range(2):
             for n in range(3):
                 c2_copy(h, s, n).wait_recv()
             parts = R2M[h, s, 0].astype(F32) + R2M[h, s, 1].astype(F32) + R2M[h, s, 2].astype(F32)
-            FIN[...] = A1[s, last_at[s]] + parts
+            FIN[...] = A1[h, s, 0].astype(F32) + parts
             for g in range(2):
                 n = s * 2 + g
                 mixed = FIN[g * ROWS : (g + 1) * ROWS, :] + NEWCTX[h, n * ROWS : (n + 1) * ROWS, :HD]
@@ -620,13 +618,13 @@
         at_step(3, of(w_wait, 1), attend_new)
         at_step(4, of(q_along, 1))
         at_step(5, of(q_share, 0))
-        at_step(6, of(q_wait, 0), pages(0, 0, 4))
-        at_step(7, pages(0, 4, 8))
-        at_step(8, pages(0, 8, 12), of(c0, 0), of(q_share, 1))
-        at_step(9, of(c1, 0), of(q_wait, 1), pages(1, 0, 2))
-        at_step(10, pages(1, 2, 5))
-        at_step(11, of(c2, 0), pages(1, 5, 8))
-        at_step(12, pages(1, 8, 10))
+        at_step(6, of(q_wait, 0), pages(0, 0, 6))
+        at_step(7, pages(0, 6, 12), of(c0, 0))
+        at_step(8, of(c1, 0), of(q_share, 1))
+        at_step(9, of(q_wait, 1), pages(1, 0, 3))
+        at_step(10, of(c2, 0), pages(1, 3, 6))
+        at_step(11, pages(1, 6, 8))
+        at_step(12, of(c3, 0), pages(1, 8, 10))
         at_step(13, pages(1, 10, 12))
         return carry
 
@@ -635,10 +633,9 @@
         for s in range(2):
             c0_copy(0, s, o).wait_send()
     c0(1)
-    c3(0)
     c1(1)
+    c4(0)
     c2(1)
-    c4(0)
     c3(1)
     c4(1)
 
@@ -708,8 +705,7 @@
         pltpu.VMEM((2, 2, 4, HALF, HD), BF16),
         pltpu.VMEM((2, 2, 2, 4, HALF, HD), BF16),
         pltpu.VMEM((2, 2, 2, 4, HALF, HD), BF16),
-        pltpu.VMEM((2, 4, HALF, HD), F32),
-        pltpu.VMEM((2, 2, 3, HALF, HD), BF16),
+        pltpu.VMEM((2, 2, 4, HALF, HD), BF16),
         pltpu.VMEM((2, 2, 3, HALF, HD), BF16),
         pltpu.VMEM((HALF, HD), F32),
         pltpu.VMEM((24, HD), jnp.int32),

time: 109 us -> 106 us (0.972)
  Pallas kernels: 107 us -> 104 us
    pallas_call x1, Pallas kernels: 107 us -> 104 us  [local(): pl.pallas_call(kernel, out_shape=jax.ShapeDtypeStruct((ROWS, 2 * GROUP *...]
where the time goes in v4:
time: 106 us
  Pallas kernels  104 us (98%)
  local copies, waits for them, and re-layouts  1.67 us (2%)
    pallas_call x1, Pallas kernels, local(): pl.pallas_call(kernel, out_shape=jax.ShapeDtypeStruct((ROWS, 2 * GROUP *...  104 us

profile of v4, /device:TPU:1, one launch (start us, length us, event | category | flops | bytes accessed | tf_op | source)
XLA Modules:
  0.0 106.0 jit_solution(13553715220596999045)
XLA Ops:
  0.0 104.3 %shard_map.136 = bf16[128,1024]{1,0:T(8,128)(2,1)} custom-call(s32[16,32]{1,0:T(8,128)} %bitcast.5, s32[32]{0:T(128)} %lengths.1, bf16[12,128,1280]{2,1,0:T(8,128)(2,1)} %store.1, bf16[128,1280]{1,0:T(8,128)(2,1)} %new_hidden.1, bf16[5120,1024]{1,0:T(8,128)(2,1)} %wq.1, bf16[5120,256]{1,0:T(8,128)(2,1)} %wk.1, bf16[5120,256]{1,0:T(8,128)(2,1)} %wv.1, ...), custom_call_target="tpu_custom_call" | custom-call | flops 12000000000 | bytes 25000000 | tf_op jit(solution)/shard_map/pallas_call | solution.py:730
  104.4 1.7 %copy.16 = bf16[128,1024]{1,0:T(8,128)(2,1)} copy(bf16[128,1024]{1,0:T(8,128)(2,1)} %shard_map.136) | data formatting | bytes 524288

commit v5 on v4

--- a/solution.py
+++ b/solution.py
@@ -335,6 +335,7 @@
     nh_ring.forward_left()
     nh_ring.forward_right()
     w_share(0)
+    w_start(1)
     w_wait(0)
 
     def product(i, slot):
@@ -583,9 +584,54 @@
 
     opposite(0)
     opposite(1)
-    w_start(1)
     project_new(1)
     project_new(3)
+
+    def drain_start():
+        for kv in range(2):
+            for h in range(2):
+                for e in (1, 2, 3):
+                    w1_copy(e, h, kv).wait_send()
+                w_spread[h][kv].drain()
+                for n in range(4):
+                    w3_copy(h, kv, c, n).wait_send()
+        nh_ring.drain()
+        for e in (1, 2, 3):
+            rcopy(SSQ.at[z], SSQ.at[z], sqs.at[e], sqr.at[e], zdev[e]).wait_send()
+
+    def drain_queries():
+        for h in range(2):
+            for s in range(2):
+                q1[h][s].drain()
+                q2[h][s].drain()
+                for n in range(4):
+                    q3_copy(h, s, c, n).wait_send()
+
+    def drain_pages():
+        def one(i, carry):
+            for s in range(2):
+                opp_copy(i, s).wait_send()
+                mid_copy(i, s).wait_send()
+            return carry
+
+        lax.fori_loop(0, ITEMS, one, 0)
+
+    def drain_c0(h):
+        for o in range(4):
+            for s in range(2):
+                c0_copy(h, s, o).wait_send()
+
+    def drain_c1(h):
+        for s in range(2):
+            for d in range(2):
+                c1o_copy(h, s, d).wait_send()
+                for n in range(2):
+                    c1m_copy(h, s, d, n).wait_send()
+
+    def drain_c2(h):
+        for s in range(2):
+            for n in range(3):
+                c2_copy(h, s, n).wait_send()
 
     def step(i, carry):
         def at_step(k, *actions):
@@ -624,54 +670,25 @@
         at_step(9, of(q_wait, 1), pages(1, 0, 3))
         at_step(10, of(c2, 0), pages(1, 3, 6))
         at_step(11, pages(1, 6, 8))
-        at_step(12, of(c3, 0), pages(1, 8, 10))
+        at_step(12, of(drain_c0, 0), of(c3, 0), pages(1, 8, 10))
         at_step(13, pages(1, 10, 12))
         return carry
 
     lax.fori_loop(0, ITEMS + 2, step, 0)
-    for o in range(4):
-        for s in range(2):
-            c0_copy(0, s, o).wait_send()
     c0(1)
     c1(1)
+    drain_start()
     c4(0)
+    drain_c1(0)
     c2(1)
+    drain_queries()
+    drain_pages()
+    drain_c2(0)
     c3(1)
+    drain_c0(1)
+    drain_c1(1)
     c4(1)
-
-    for kv in range(2):
-        for h in range(2):
-            for e in (1, 2, 3):
-                w1_copy(e, h, kv).wait_send()
-            w_spread[h][kv].drain()
-            for n in range(4):
-                w3_copy(h, kv, c, n).wait_send()
-    nh_ring.drain()
-    for e in (1, 2, 3):
-        rcopy(SSQ.at[z], SSQ.at[z], sqs.at[e], sqr.at[e], zdev[e]).wait_send()
-
-    def drain(i, carry):
-        for s in range(2):
-            opp_copy(i, s).wait_send()
-            mid_copy(i, s).wait_send()
-        return carry
-
-    lax.fori_loop(0, ITEMS, drain, 0)
-    for o in range(4):
-        for s in range(2):
-            c0_copy(1, s, o).wait_send()
-    for h in range(2):
-        for s in range(2):
-            q1[h][s].drain()
-            q2[h][s].drain()
-            for n in range(4):
-                q3_copy(h, s, c, n).wait_send()
-            for d in range(2):
-                c1o_copy(h, s, d).wait_send()
-                for n in range(2):
-                    c1m_copy(h, s, d, n).wait_send()
-            for n in range(3):
-                c2_copy(h, s, n).wait_send()
+    drain_c2(1)
 
 
 def local(store, new_hidden, wq, wk, wv, norm_gain, q_gain, k_gain, page_table, hist_len):

time: 106 us -> 106 us (level)
  no operation moved by 1% of the time
where the time goes in v5:
time: 106 us
  Pallas kernels  104 us (98%)
  local copies, waits for them, and re-layouts  1.67 us (2%)
    pallas_call x1, Pallas kernels, local(): pl.pallas_call(kernel, out_shape=jax.ShapeDtypeStruct((ROWS, 2 * GROUP *...  104 us

profile of v5, /device:TPU:1, one launch (start us, length us, event | category | flops | bytes accessed | tf_op | source)
XLA Modules:
  0.0 105.6 jit_solution(17987536456532216518)
XLA Ops:
  0.0 103.9 %shard_map.136 = bf16[128,1024]{1,0:T(8,128)(2,1)} custom-call(s32[16,32]{1,0:T(8,128)} %bitcast.5, s32[32]{0:T(128)} %lengths.1, bf16[12,128,1280]{2,1,0:T(8,128)(2,1)} %store.1, bf16[128,1280]{1,0:T(8,128)(2,1)} %new_hidden.1, bf16[5120,1024]{1,0:T(8,128)(2,1)} %wq.1, bf16[5120,256]{1,0:T(8,128)(2,1)} %wk.1, bf16[5120,256]{1,0:T(8,128)(2,1)} %wv.1, ...), custom_call_target="tpu_custom_call" | custom-call | flops 12000000000 | bytes 25000000 | tf_op jit(solution)/shard_map/pallas_call | solution.py:747
  103.9 1.7 %copy.16 = bf16[128,1024]{1,0:T(8,128)(2,1)} copy(bf16[128,1024]{1,0:T(8,128)(2,1)} %shard_map.136) | data formatting | bytes 524288
